TPU v7x, 32 devices: a whole 2x2x4 slice. The times are simulated.
32 devices in a mesh: wide: 8 (over y, x, core), narrow: 4 (over z).
Axes of the slice: x: 2, y: 2, z: 4, core: 2. Of those that a mesh axis runs over, the one named last changes fastest.
Arguments:
- tokens: bfloat16 [32, 1024, 1024], P(('wide', 'narrow')), may hold values from -6 to 6
- lengths: int32 [32, 8], P(('wide', 'narrow')), may hold values from 1 to 256, 1024 in all within a row
- ln1_gain: bfloat16 [1024], P('narrow'), may hold values from 0.5 to 1.5
- ln1_bias: bfloat16 [1024], P('narrow'), may hold values from -2 to 2
- w_query: bfloat16 [1024, 1024], P('narrow'), may hold values from -0.1875 to 0.1875
- w_key: bfloat16 [1024, 1024], P('narrow'), may hold values from -0.1875 to 0.1875
- w_value: bfloat16 [1024, 1024], P('narrow'), may hold values from -0.1875 to 0.1875
- w_out: bfloat16 [1024, 1024], P('narrow'), may hold values from -0.75 to 0.75
- ln2_gain: bfloat16 [1024], P('narrow'), may hold values from 0.5 to 1.5
- ln2_bias: bfloat16 [1024], P('narrow'), may hold values from -2 to 2
- w_gate: bfloat16 [1024, 4096], P('narrow'), may hold values from -0.1875 to 0.1875
- w_up: bfloat16 [1024, 4096], P('narrow'), may hold values from -0.1875 to 0.1875
- w_down: bfloat16 [4096, 1024], P('narrow'), may hold values from -0.09375 to 0.09375
- cotangent: bfloat16 [32, 1024, 1024], P(('wide', 'narrow')), may hold values from -6 to 6
Outputs:
- output: bfloat16 [32, 1024, 1024], P(('wide', 'narrow'))
- input_grad: float32 [32, 1024, 1024], P(('wide', 'narrow'))
- grad_ln1_gain: float32 [1024], P('narrow')
- grad_ln1_bias: float32 [1024], P('narrow')
- grad_query: float32 [1024, 1024], P('narrow')
- grad_key: float32 [1024, 1024], P('narrow')
- grad_value: float32 [1024, 1024], P('narrow')
- grad_out: float32 [1024, 1024], P('narrow')
- grad_ln2_gain: float32 [1024], P('narrow')
- grad_ln2_bias: float32 [1024], P('narrow')
- grad_gate: float32 [1024, 4096], P('narrow')
- grad_up: float32 [1024, 4096], P('narrow')
- grad_down: float32 [4096, 1024], P('narrow')
Inputs may be any that keep to these rules, and one draw needn't show every extreme that they name: Each row's 8 window lengths sum to 1024; in every row the longest window has exactly 256 tokens.
All inputs are finite; a program needn't handle non-finite values.
Results may differ from a plain program's by a relative error of at most 0.017.
Values may be sent and summed in bfloat16 or wider, within the bound.
A program may use at most 320 MiB of HBM per device.

v0:
```python
import math

import jax
import jax.numpy as jnp
from jax import lax
from jax.sharding import PartitionSpec as P

HEAD = 64


epsilon = 1e-05
rotary_base = 10000.0
masked_score = -1e30


def for_sending(shard):
    return jax.tree.map(lambda a: a.astype(jnp.bfloat16) if a.dtype == jnp.float32 else a, shard)


def segments_positions(lengths, row_len):
    ends = jnp.cumsum(lengths, axis=-1)
    starts = ends - lengths
    places = jnp.arange(row_len, dtype=jnp.int32)
    inside = (places[None, :, None] >= starts[:, None, :]) & (
        places[None, :, None] < ends[:, None, :]
    )
    numbers = jnp.arange(lengths.shape[-1], dtype=jnp.int32)
    segment = jnp.sum(jnp.where(inside, numbers[None, None, :], 0), axis=-1)
    offset = jnp.sum(jnp.where(inside, starts[:, None, :], 0), axis=-1)
    return (segment, places[None, :] - offset)


def rotary_tables(position, head_size):
    half_size = head_size // 2
    exponent = jnp.arange(half_size, dtype=jnp.float32) * (-2.0 / head_size)
    inverse = jnp.power(jnp.float32(rotary_base), exponent)
    angles = position.astype(jnp.float32)[..., None] * inverse
    angles = jnp.concatenate([angles, angles], axis=-1)
    return (jnp.cos(angles)[..., None, :], jnp.sin(angles)[..., None, :])


def turn(source, cos_table, sin_table):
    half_size = source.shape[-1] // 2
    rotated = jnp.concatenate([-source[..., half_size:], source[..., :half_size]], axis=-1)
    return source * cos_table + rotated * sin_table


def unturn(gradient, cos_table, sin_table):
    half_size = gradient.shape[-1] // 2
    scaled = gradient * sin_table
    back_part = jnp.concatenate([scaled[..., half_size:], -scaled[..., :half_size]], axis=-1)
    return gradient * cos_table + back_part


def normalize(source):
    center = source - jnp.mean(source, axis=-1, keepdims=True)
    inverse_std = lax.rsqrt(jnp.mean(center * center, axis=-1, keepdims=True) + epsilon)
    return (center * inverse_std, inverse_std)


def norm_back(grad_normed, normed_hat, inverse_std, gain_full):
    scaled = grad_normed * gain_full
    first_mean = jnp.mean(scaled, axis=-1, keepdims=True)
    second_mean = jnp.mean(scaled * normed_hat, axis=-1, keepdims=True)
    return inverse_std * (scaled - first_mean - normed_hat * second_mean)


def masked_scores(query_block, segment_block, keys_row, segment_row):
    scores = jnp.einsum("qhe,khe->hqk", query_block, keys_row, preferred_element_type=jnp.float32)
    scores = scores * (1.0 / math.sqrt(query_block.shape[-1]))
    same_window = segment_block[:, None] == segment_row[None, :]
    return jnp.where(same_window[None], scores, masked_score)


def split_blocks(row_array):
    length = row_array.shape[0]
    block_rows = min(512, length)
    return row_array.reshape((length // block_rows, block_rows) + row_array.shape[1:])


def attend_row(row_items):
    queries_row, keys_row, values_row, segment_row = row_items

    def one_block(block_items):
        query_block, segment_block = block_items
        scores = masked_scores(query_block, segment_block, keys_row, segment_row)
        highest = jnp.max(scores, axis=-1, keepdims=True)
        raised = jnp.exp(scores - highest)
        summed = jnp.sum(raised, axis=-1, keepdims=True)
        weights_low = (raised / summed).astype(jnp.bfloat16)
        result = jnp.einsum(
            "hqk,khe->qhe", weights_low, values_row, preferred_element_type=jnp.float32
        )
        return (result, (highest + jnp.log(summed))[..., 0])

    results, logsums = lax.map(one_block, (split_blocks(queries_row), split_blocks(segment_row)))
    return (results.reshape(queries_row.shape), logsums)


def attend_row_back(row_items):
    queries_row, keys_row, values_row, segment_row, grad_row, logsum_row = row_items
    score_scale = 1.0 / math.sqrt(queries_row.shape[-1])

    def one_block(carry, block_items):
        grad_keys_acc, grad_values_acc = carry
        query_block, segment_block, grad_block, logsum_block = block_items
        scores = masked_scores(query_block, segment_block, keys_row, segment_row)
        probability = jnp.exp(scores - logsum_block[..., None])
        grad_probs = jnp.einsum(
            "qhe,khe->hqk", grad_block, values_row, preferred_element_type=jnp.float32
        )
        row_dot = jnp.sum(probability * grad_probs, axis=-1, keepdims=True)
        grad_scores = (probability * (grad_probs - row_dot)).astype(jnp.bfloat16)
        grad_query_block = (
            jnp.einsum("hqk,khe->qhe", grad_scores, keys_row, preferred_element_type=jnp.float32)
            * score_scale
        )
        grad_keys_acc = (
            grad_keys_acc
            + jnp.einsum(
                "hqk,qhe->khe", grad_scores, query_block, preferred_element_type=jnp.float32
            )
            * score_scale
        )
        grad_values_acc = grad_values_acc + jnp.einsum(
            "hqk,qhe->khe",
            probability.astype(jnp.bfloat16),
            grad_block,
            preferred_element_type=jnp.float32,
        )
        return ((grad_keys_acc, grad_values_acc), grad_query_block)

    zero_grads = jnp.zeros(keys_row.shape, jnp.float32)
    block_items = (
        split_blocks(queries_row),
        split_blocks(segment_row),
        split_blocks(grad_row),
        logsum_row,
    )
    (grad_keys_row, grad_values_row), grad_queries_blocks = lax.scan(
        one_block, (zero_grads, zero_grads), block_items
    )
    return (grad_queries_blocks.reshape(queries_row.shape), grad_keys_row, grad_values_row)


def shards(
    tokens,
    lengths,
    ln1_gain,
    ln1_bias,
    w_query,
    w_key,
    w_value,
    w_out,
    ln2_gain,
    ln2_bias,
    w_gate,
    w_up,
    w_down,
    cotangent,
):
    rows_here, row_len, features = tokens.shape
    heads_count = features // HEAD
    head_shape = (rows_here, row_len, heads_count, HEAD)
    gain_one, bias_one, query_full, key_full, value_full, out_full = (
        lax.all_gather(ln1_gain, "narrow", axis=0, tiled=True),
        lax.all_gather(ln1_bias, "narrow", axis=0, tiled=True),
        lax.all_gather(w_query, "narrow", axis=0, tiled=True),
        lax.all_gather(w_key, "narrow", axis=0, tiled=True),
        lax.all_gather(w_value, "narrow", axis=0, tiled=True),
        lax.all_gather(w_out, "narrow", axis=0, tiled=True),
    )
    gain_two, bias_two, gate_full, up_full, down_full = (
        lax.all_gather(ln2_gain, "narrow", axis=0, tiled=True),
        lax.all_gather(ln2_bias, "narrow", axis=0, tiled=True),
        lax.all_gather(w_gate, "narrow", axis=0, tiled=True),
        lax.all_gather(w_up, "narrow", axis=0, tiled=True),
        lax.all_gather(w_down, "narrow", axis=0, tiled=True),
    )
    segment, position = segments_positions(lengths, row_len)
    cos_table, sin_table = rotary_tables(position, HEAD)
    tokens_flat = tokens.reshape(rows_here * row_len, features).astype(jnp.float32)
    hat_one, inverse_one = normalize(tokens_flat)
    normed_one = (hat_one * gain_one.astype(jnp.float32) + bias_one.astype(jnp.float32)).astype(
        jnp.bfloat16
    )
    queries_pre = jnp.dot(normed_one, query_full, preferred_element_type=jnp.float32).reshape(
        head_shape
    )
    keys_pre = jnp.dot(normed_one, key_full, preferred_element_type=jnp.float32).reshape(head_shape)
    queries_rot = turn(queries_pre, cos_table, sin_table).astype(jnp.bfloat16)
    keys_rot = turn(keys_pre, cos_table, sin_table).astype(jnp.bfloat16)
    values_low = (
        jnp.dot(normed_one, value_full, preferred_element_type=jnp.float32)
        .astype(jnp.bfloat16)
        .reshape(head_shape)
    )
    attended, logsum_rows = lax.map(attend_row, (queries_rot, keys_rot, values_low, segment))
    attended_low = attended.reshape(rows_here * row_len, features).astype(jnp.bfloat16)
    mixed = tokens_flat + jnp.dot(attended_low, out_full, preferred_element_type=jnp.float32)
    hat_two, inverse_two = normalize(mixed)
    normed_two = (hat_two * gain_two.astype(jnp.float32) + bias_two.astype(jnp.float32)).astype(
        jnp.bfloat16
    )
    gate_pre = jnp.dot(normed_two, gate_full, preferred_element_type=jnp.float32)
    up_pre = jnp.dot(normed_two, up_full, preferred_element_type=jnp.float32)
    sigmoid_gate = jax.nn.sigmoid(gate_pre)
    silu_gate = gate_pre * sigmoid_gate
    hidden = (silu_gate * up_pre).astype(jnp.bfloat16)
    final = mixed + jnp.dot(hidden, down_full, preferred_element_type=jnp.float32)
    output = final.astype(jnp.bfloat16).reshape(tokens.shape)
    gain_two, bias_two, gate_full, up_full, down_full = (
        lax.all_gather(ln2_gain, "narrow", axis=0, tiled=True),
        lax.all_gather(ln2_bias, "narrow", axis=0, tiled=True),
        lax.all_gather(w_gate, "narrow", axis=0, tiled=True),
        lax.all_gather(w_up, "narrow", axis=0, tiled=True),
        lax.all_gather(w_down, "narrow", axis=0, tiled=True),
    )
    cotangent_flat = cotangent.reshape(rows_here * row_len, features)
    grad_down = jnp.einsum("tf,td->fd", hidden, cotangent_flat, preferred_element_type=jnp.float32)
    grad_hidden = jnp.einsum(
        "td,fd->tf", cotangent_flat, down_full, preferred_element_type=jnp.float32
    )
    grad_gate_pre = (
        grad_hidden * up_pre * sigmoid_gate * (1.0 + gate_pre * (1.0 - sigmoid_gate))
    ).astype(jnp.bfloat16)
    grad_up_pre = (grad_hidden * silu_gate).astype(jnp.bfloat16)
    grad_gate = jnp.einsum(
        "td,tf->df", normed_two, grad_gate_pre, preferred_element_type=jnp.float32
    )
    grad_up = jnp.einsum("td,tf->df", normed_two, grad_up_pre, preferred_element_type=jnp.float32)
    grad_normed_two = jnp.einsum(
        "tf,df->td", grad_gate_pre, gate_full, preferred_element_type=jnp.float32
    )
    grad_normed_two = grad_normed_two + jnp.einsum(
        "tf,df->td", grad_up_pre, up_full, preferred_element_type=jnp.float32
    )
    grad_gain_two = jnp.sum(grad_normed_two * hat_two, axis=0)
    grad_bias_two = jnp.sum(grad_normed_two, axis=0)
    grad_mixed = cotangent_flat.astype(jnp.float32) + norm_back(
        grad_normed_two, hat_two, inverse_two, gain_two.astype(jnp.float32)
    )
    ffn_grads = (grad_gain_two, grad_bias_two, grad_gate, grad_up, grad_down)
    gain_one, bias_one, query_full, key_full, value_full, out_full = (
        lax.all_gather(ln1_gain, "narrow", axis=0, tiled=True),
        lax.all_gather(ln1_bias, "narrow", axis=0, tiled=True),
        lax.all_gather(w_query, "narrow", axis=0, tiled=True),
        lax.all_gather(w_key, "narrow", axis=0, tiled=True),
        lax.all_gather(w_value, "narrow", axis=0, tiled=True),
        lax.all_gather(w_out, "narrow", axis=0, tiled=True),
    )
    grad_res = grad_mixed.astype(jnp.bfloat16)
    grad_out = jnp.einsum("td,te->de", attended_low, grad_res, preferred_element_type=jnp.float32)
    grad_attended = (
        jnp.einsum("te,de->td", grad_res, out_full, preferred_element_type=jnp.float32)
        .astype(jnp.bfloat16)
        .reshape(head_shape)
    )
    grad_queries_rot, grad_keys_rot, grad_values = lax.map(
        attend_row_back, (queries_rot, keys_rot, values_low, segment, grad_attended, logsum_rows)
    )
    flat_shape = (rows_here * row_len, features)
    grad_queries = (
        unturn(grad_queries_rot, cos_table, sin_table).astype(jnp.bfloat16).reshape(flat_shape)
    )
    grad_keys = unturn(grad_keys_rot, cos_table, sin_table).astype(jnp.bfloat16).reshape(flat_shape)
    grad_values_low = grad_values.astype(jnp.bfloat16).reshape(flat_shape)
    grad_query = jnp.einsum(
        "td,te->de", normed_one, grad_queries, preferred_element_type=jnp.float32
    )
    grad_key = jnp.einsum("td,te->de", normed_one, grad_keys, preferred_element_type=jnp.float32)
    grad_value = jnp.einsum(
        "td,te->de", normed_one, grad_values_low, preferred_element_type=jnp.float32
    )
    grad_normed_one = jnp.einsum(
        "te,de->td", grad_queries, query_full, preferred_element_type=jnp.float32
    )
    grad_normed_one = grad_normed_one + jnp.einsum(
        "te,de->td", grad_keys, key_full, preferred_element_type=jnp.float32
    )
    grad_normed_one = grad_normed_one + jnp.einsum(
        "te,de->td", grad_values_low, value_full, preferred_element_type=jnp.float32
    )
    grad_gain_one = jnp.sum(grad_normed_one * hat_one, axis=0)
    grad_bias_one = jnp.sum(grad_normed_one, axis=0)
    input_grad = grad_mixed + norm_back(
        grad_normed_one, hat_one, inverse_one, gain_one.astype(jnp.float32)
    )
    all_parts = jax.tree.map(
        lambda part: part.astype(jnp.float32),
        lax.psum_scatter(
            for_sending(
                (grad_gain_one, grad_bias_one, grad_query, grad_key, grad_value, grad_out)
                + ffn_grads
            ),
            "narrow",
            scatter_dimension=0,
            tiled=True,
        ),
    )
    weight_done = tuple(lax.psum(tuple(all_parts), "wide"))
    return (output, input_grad.reshape(tokens.shape)) + weight_done


def solution(mesh):
    placed = (
        P(("wide", "narrow"), None, None),
        P(("wide", "narrow"), None),
        P("narrow"),
        P("narrow"),
        P("narrow", None),
        P("narrow", None),
        P("narrow", None),
        P("narrow", None),
        P("narrow"),
        P("narrow"),
        P("narrow", None),
        P("narrow", None),
        P("narrow", None),
        P(("wide", "narrow"), None, None),
    )
    return jax.shard_map(
        shards,
        mesh=mesh,
        in_specs=placed,
        out_specs=(
            P(("wide", "narrow"), None, None),
            P(("wide", "narrow"), None, None),
            P("narrow"),
            P("narrow"),
            P("narrow", None),
            P("narrow", None),
            P("narrow", None),
            P("narrow", None),
            P("narrow"),
            P("narrow"),
            P("narrow", None),
            P("narrow", None),
            P("narrow", None),
        ),
        check_vma=False,
    )
```

profile of v0, /device:TPU:0, one launch (start us, length us, event | category | flops | bytes accessed | tf_op | source)
XLA Modules:
  0.0 1947.7 jit_solution(3481099664080673898)
XLA Ops:
  12.5 12.7 all-gather.3
  25.8 7.6 all-gather.2
  34.0 10.6 all-gather.1
  44.6 7.8 all-gather
  71.7 6.6 reshape.748
  110.9 40.1 %all-gather.16.cloned.1.call-done = bf16[1024,1024]{1,0:T(8,128)(2,1)} async-done(((bf16[256,1024]{1,0:T(8,128)(2,1)}), bf16[1024,1024]{1,0:T(8,128)(2,1)}) %all-gather.16.cloned.1.call-update) | async-done | bytes 2097168 | tf_op jit(solution)/shard_map/all_gather | solution.py:170
  157.3 94.9 %while.47 = (s32[]{:T(128)}, bf16[2,512,16,64]{1,3,2,0:T(8,128)(2,1)}, f32[2,16,512]{2,1,0:T(8,128)S(1)}, s32[2,512]{1,0:T(2,128)S(1)}, s32[1024]{0:T(1024)S(1)}...) while((s32[]{:T(128)}, ...), condition=%wide.region_8.9_spmd, body=%wide.region_5.8_spmd.sunk | while | flops 2248663040 | bytes 135538864 | solution.py:96
  157.6 15.5 fusion.143
  173.1 15.4 fusion.144
  188.6 14.6 bitcast_dynamic-update-slice_fusion.4
  204.9 15.6 fusion.143
  220.5 15.4 fusion.144
  235.9 14.7 bitcast_dynamic-update-slice_fusion.4
  267.2 79.9 %all-gather.22.cloned.1.call-done = bf16[1024,4096]{1,0:T(8,128)(2,1)} async-done(((bf16[256,4096]{1,0:T(8,128)(2,1)}), bf16[1024,4096]{1,0:T(8,128)(2,1)}) %all-gather.22.cloned.1.call-update) | async-done | bytes 8388624 | tf_op jit(solution)/shard_map/all_gather | solution.py:177
  347.1 16.1 fusion.84
  363.2 133.2 %all-gather.20.cloned.1.call-done = bf16[1024,4096]{1,0:T(8,128)(2,1)} async-done(((bf16[256,4096]{1,0:T(8,128)(2,1)}), bf16[1024,4096]{1,0:T(8,128)(2,1)}) %all-gather.20.cloned.1.call-update) | async-done | bytes 8388624 | tf_op jit(solution)/shard_map/all_gather | solution.py:176
  496.4 16.3 fusion.83
  512.7 133.1 %all-gather.24.cloned.1.call-done = bf16[4096,1024]{1,0:T(8,128)(2,1)} async-done(((bf16[1024,1024]{1,0:T(8,128)(2,1)}), bf16[4096,1024]{1,0:T(8,128)(2,1)}) %all-gather.24.cloned.1.call-update) | async-done | bytes 8388624 | tf_op jit(solution)/shard_map/all_gather | solution.py:178
  645.9 30.4 %multiply_convert_fusion.1 = (bf16[1024,4096]{1,0:T(8,128)(2,1)}, bf16[1024,4096]{1,0:T(8,128)(2,1)}, bf16[1024,4096]{1,0:T(8,128)(2,1)}) fusion(f32[1024,4096]{1,0:T(8,128)} %fusion.83, f32[1024,4096]{1,0:T(8,128)} %fusion.84, bf16[4096,1024]{1,0:T(8,128)(2,1)} %all-gather.24.cloned.1.call-done, bf16[1,1024,1024]{2,1,0:T(8,128)(2,1)} %param.31), kind=kOutput, calls=%fused_computation.44 | convolution fusion | flops 8652849152 | bytes 69206016 | tf_op jit(solution)/shard_map/td,fd->tf/dot_general | solution.py:221
  676.3 15.7 fusion.85
  692.0 14.0 multiply_reduce_fusion.1
  713.2 6.6 convolution_convert_fusion.7
  719.7 6.4 reshape.770
  731.6 296.3 %while.48 = (s32[]{:T(128)}, f32[1024,16,64]{0,2,1:T(8,128)}, f32[1024,16,64]{0,2,1:T(8,128)}, f32[2,512,16,64]{1,0,3,2:T(2,128)}, bf16[2,512,16,64]{1,3,2,0:T(8...) while((s32[]{:T(128)}, f32[1024,16,64]{0,2,1:T(8,128)}, ...), condition=%wide.region_15.16_spmd.clone, body=%wide.region_13.15_spmd.clone.sunk | while | flops 5500821504 | bytes 384018720 | solution.py:140
  732.1 14.9 fusion.154
  747.0 17.7 bitcast_add_fusion.6
  764.7 25.9 %multiply_reduce_fusion.7 = (f32[16,512]{1,0:T(8,128)S(1)}, f32[16,512,1024]{2,1,0:T(8,128)}) fusion(f32[16,512,1024]{2,1,0:T(8,128)} %fusion.154, f32[16,512]{1,0:T(8,128)S(1)} %dynamic-slice_bitcast_fusion.2, pred[512,1024]{1,0:T(8,128)(4,1)S(1)} %broadcast_compare_fusion.5, bf16[1024,16,64]{0,2,1:T(8,128)(2,1)} %get-tuple-element.604, ...), kind=kOutput, calls=%fused_computation.17.clone.1 | convolution fusion | flops 1115676672 | bytes 70844416 | tf_op jit(solution)/shard_map/while/body/eval_jaxpr/while/body/eval_jaxpr/qhe,khe->hqk/dot_general | solution.py:109
  790.6 27.8 %multiply_convert_fusion.5 = bf16[16,512,1024]{2,1,0:T(8,128)(2,1)} fusion(f32[16,512,1024]{2,1,0:T(8,128)} %get-tuple-element.539, f32[16,512,1024]{2,1,0:T(8,128)} %fusion.154, f32[16,512]{1,0:T(8,128)S(1)} %get-tuple-element.540, f32[16,512]{1,0:T(8,128)S(1)} %dynamic-slice_bitcast_fusion.2, pred[512,1024]{1,0:T(8,128)(4,1)S(1)} %broadcast_compare_fusion.5), kind=kLoop, calls=%fused_computation.16.clone.1 | loop fusion | flops 50331648 | bytes 84475904 | tf_op jit(solution)/shard_map/while/body/eval_jaxpr/while/body/eval_jaxpr/convert_element_type | solution.py:113
  818.4 10.6 multiply_bitcast_fusion.3
  830.3 6.6 bitcast_add_fusion.5
  840.4 38.1 %dynamic_update_slice.31 = f32[2,512,16,64]{1,0,3,2:T(2,128)} dynamic-update-slice(f32[2,512,16,64]{1,0,3,2:T(2,128)} %get-tuple-element.584, f32[1,512,16,64]{1,0,3,2:T(1,128)} %copy.115, s32[]{:T(128)S(6)} %copy.132, s32[]{:T(128)} %constant.97.clone.1..sunk, s32[]{:T(128)} %constant.97.clone.1..sunk, s32[]{:T(128)} %constant.97.clone.1..sunk) | dynamic-update-slice | bytes 4194308 | tf_op jit(solution)/shard_map/while/body/eval_jaxpr/while/body/jit(dynamic_update_index_in_dim)/dynamic_update_slice | solution.py:96
  878.9 14.7 fusion.154
  893.7 18.7 bitcast_add_fusion.6
  912.4 25.9 %multiply_reduce_fusion.7 = (f32[16,512]{1,0:T(8,128)S(1)}, f32[16,512,1024]{2,1,0:T(8,128)}) fusion(f32[16,512,1024]{2,1,0:T(8,128)} %fusion.154, f32[16,512]{1,0:T(8,128)S(1)} %dynamic-slice_bitcast_fusion.2, pred[512,1024]{1,0:T(8,128)(4,1)S(1)} %broadcast_compare_fusion.5, bf16[1024,16,64]{0,2,1:T(8,128)(2,1)} %get-tuple-element.604, ...), kind=kOutput, calls=%fused_computation.17.clone.1 | convolution fusion | flops 1115676672 | bytes 70844416 | tf_op jit(solution)/shard_map/while/body/eval_jaxpr/while/body/eval_jaxpr/qhe,khe->hqk/dot_general | solution.py:109
  938.3 27.8 %multiply_convert_fusion.5 = bf16[16,512,1024]{2,1,0:T(8,128)(2,1)} fusion(f32[16,512,1024]{2,1,0:T(8,128)} %get-tuple-element.539, f32[16,512,1024]{2,1,0:T(8,128)} %fusion.154, f32[16,512]{1,0:T(8,128)S(1)} %get-tuple-element.540, f32[16,512]{1,0:T(8,128)S(1)} %dynamic-slice_bitcast_fusion.2, pred[512,1024]{1,0:T(8,128)(4,1)S(1)} %broadcast_compare_fusion.5), kind=kLoop, calls=%fused_computation.16.clone.1 | loop fusion | flops 50331648 | bytes 84475904 | tf_op jit(solution)/shard_map/while/body/eval_jaxpr/while/body/eval_jaxpr/convert_element_type | solution.py:113
  966.1 10.6 multiply_bitcast_fusion.3
  978.0 7.9 bitcast_add_fusion.5
  989.4 38.1 %dynamic_update_slice.31 = f32[2,512,16,64]{1,0,3,2:T(2,128)} dynamic-update-slice(f32[2,512,16,64]{1,0,3,2:T(2,128)} %get-tuple-element.584, f32[1,512,16,64]{1,0,3,2:T(1,128)} %copy.115, s32[]{:T(128)S(6)} %copy.132, s32[]{:T(128)} %constant.97.clone.1..sunk, s32[]{:T(128)} %constant.97.clone.1..sunk, s32[]{:T(128)} %constant.97.clone.1..sunk) | dynamic-update-slice | bytes 4194308 | tf_op jit(solution)/shard_map/while/body/eval_jaxpr/while/body/jit(dynamic_update_index_in_dim)/dynamic_update_slice | solution.py:96
  1035.8 6.8 broadcast_in_dim.100
  1066.1 15.0 convolution_convert_fusion.2
  1081.1 14.7 convolution_convert_fusion.1
  1095.9 15.3 convolution_convert_fusion
  1113.1 15.4 fusion.59
  1155.5 10.2 all-reduce.5
  1169.5 146.0 %reduce-scatter.16.cloned.1.call-done = bf16[256,4096]{1,0:T(8,128)(2,1)} async-done(((bf16[1024,4096]{1,0:T(8,128)(2,1)}), bf16[256,4096]{1,0:T(8,128)(2,1)}) %reduce-scatter.16.cloned.1.call-update) | async-done | bytes 2097168 | tf_op jit(solution)/shard_map/reduce_scatter | solution.py:291
  1315.6 147.6 %reduce-scatter.18.cloned.1.call-done = bf16[256,4096]{1,0:T(8,128)(2,1)} async-done(((bf16[1024,4096]{1,0:T(8,128)(2,1)}), bf16[256,4096]{1,0:T(8,128)(2,1)}) %reduce-scatter.18.cloned.1.call-update) | async-done | bytes 2097168 | tf_op jit(solution)/shard_map/reduce_scatter | solution.py:291
  1463.1 147.4 %reduce-scatter.20.cloned.1.call-done = bf16[1024,1024]{1,0:T(8,128)(2,1)} async-done(((bf16[4096,1024]{1,0:T(8,128)(2,1)}), bf16[1024,1024]{1,0:T(8,128)(2,1)}) %reduce-scatter.20.cloned.1.call-update) | async-done | bytes 2097168 | tf_op jit(solution)/shard_map/reduce_scatter | solution.py:291
  1610.6 330.2 %all-reduce.7 = (f32[256]{0:T(256)}, f32[256]{0:T(256)}, f32[256,1024]{1,0:T(8,128)}, f32[256,1024]{1,0:T(8,128)}, f32[256,1024]{1,0:T(8,128)}, /*index=5*/f32[2...) all-reduce(f32[256]{0:T(256)S(1)} %dynamic-slice_convert_fusion.3, ...), channel_id=1, replica_groups=mesh['wide'=8,'narrow'=4] {'wide'}, use_global_device_ids=true, to_apply=%region_20.21 | all-reduce | flops 4195328 | bytes 25174016 | tf_op jit(solution)/shard_map/psum | solution.py:301
  (236 shorter events, 168.9 us)
Async XLA Ops:
  7.2 4.8 copy-start.41
  7.2 5.2 copy-start.42
  7.2 5.2 copy-start.43
  7.2 5.2 copy-start.44
  7.2 5.2 copy-start.45
  7.2 58.1 %all-gather.12.cloned.1.call-start = ((), (), s32[]{:S(2)}) async-start(), calls=%async_computation.7 | async-start | bytes 2621440 | tf_op jit(solution)/shard_map/all_gather | solution.py:168
  8.0 96.8 %all-gather.14.cloned.1.call-start = ((), (), s32[]{:S(2)}) async-start(), calls=%async_computation.8 | async-start | bytes 2621440 | tf_op jit(solution)/shard_map/all_gather | solution.py:169
  8.7 142.3 %all-gather.16.cloned.1.call-start = ((), (), s32[]{:S(2)}) async-start(), calls=%async_computation.9 | async-start | bytes 2621440 | tf_op jit(solution)/shard_map/all_gather | solution.py:170
  9.5 248.3 %all-gather.18.cloned.1.call-start = ((), (), s32[]{:S(2)}) async-start(), calls=%async_computation.10 | async-start | bytes 2621440 | tf_op jit(solution)/shard_map/all_gather | solution.py:171
  10.0 337.1 %all-gather.22.cloned.1.call-start = ((), (), s32[]{:S(2)}) async-start(), calls=%async_computation.12 | async-start | bytes 10485760 | tf_op jit(solution)/shard_map/all_gather | solution.py:177
  10.6 485.8 %all-gather.20.cloned.1.call-start = ((), (), s32[]{:S(2)}) async-start(), calls=%async_computation.11 | async-start | bytes 10485760 | tf_op jit(solution)/shard_map/all_gather | solution.py:176
  11.2 634.7 %all-gather.24.cloned.1.call-start = ((), (), s32[]{:S(2)}) async-start(), calls=%async_computation.13 | async-start | bytes 10485760 | tf_op jit(solution)/shard_map/all_gather | solution.py:178
  11.9 1154.1 %reduce-scatter.14.cloned.1.call-start = ((), (), s32[]{:S(2)}) async-start(), calls=%async_computation.17 | async-start | bytes 2621440 | tf_op jit(solution)/shard_map/reduce_scatter | solution.py:291
  44.6 106.4 %copy-start.34 = (f32[4,1,256]{2,1,0:T(1,128)}, f32[4,1,256]{2,1,0:T(1,128)S(1)}, u32[]{:S(2)}) copy-start(f32[4,1,256]{2,1,0:T(1,128)S(1)} %convert_element_type.248) | copy-start | bytes 12292
  52.4 98.6 %copy-start.29 = (f32[4,1,256]{2,1,0:T(1,128)}, f32[4,1,256]{2,1,0:T(1,128)S(1)}, u32[]{:S(2)}) copy-start(f32[4,1,256]{2,1,0:T(1,128)S(1)} %convert_element_type.247) | copy-start | bytes 12292
  53.6 56.1 %copy-start.15 = (f32[1024,64]{0,1:T(8,128)}, f32[1024,64]{0,1:T(8,128)S(1)}, u32[]{:S(2)}) copy-start(f32[1024,64]{0,1:T(8,128)S(1)} %get-tuple-element.407) | copy-start | bytes 786436
  53.6 56.1 %copy-start.17 = (f32[1024,64]{0,1:T(8,128)}, f32[1024,64]{0,1:T(8,128)S(1)}, u32[]{:S(2)}) copy-start(f32[1024,64]{0,1:T(8,128)S(1)} %get-tuple-element.408) | copy-start | bytes 786436
  60.3 44.5 %copy-start.9 = (bf16[1,1024,1024]{1,2,0:T(8,128)(2,1)}, bf16[1,1024,1024]{1,2,0:T(8,128)(2,1)S(1)}, u32[]{:S(2)}) copy-start(bf16[1,1024,1024]{1,2,0:T(8,128)(2,1)S(1)} %copy.73) | copy-start | bytes 6291460
  60.7 90.4 %copy-start.26 = (f32[1024]{0:T(1024)}, f32[1024]{0:T(1024)S(1)}, u32[]{:S(2)}) copy-start(f32[1024]{0:T(1024)S(1)} %broadcast_multiply_fusion.8) | copy-start | bytes 12292
  61.3 89.8 %copy-start.31 = (f32[1024]{0:T(1024)}, f32[1024]{0:T(1024)S(1)}, u32[]{:S(2)}) copy-start(f32[1024]{0:T(1024)S(1)} %add_rsqrt_fusion.1) | copy-start | bytes 12292
  173.1 15.4 copy-start.4
  173.1 15.4 copy-start.21
  220.5 15.4 copy-start.4
  220.5 15.4 copy-start.21
  676.3 15.7 copy-start.7
  676.3 15.7 copy-start.47
  692.0 14.0 copy-start.14
  713.1 452.9 %reduce-scatter.12.cloned.1.call-start = ((), (), s32[]{:S(2)}) async-start(), calls=%async_computation.16 | async-start | bytes 2621440 | tf_op jit(solution)/shard_map/reduce_scatter | solution.py:291
  731.7 15.3 copy-start.1
  818.4 11.9 copy-start
  830.3 6.6 copy-start.5
  836.9 41.6 %copy-start.2 = (bf16[1024,16,64]{0,2,1:T(8,128)(2,1)S(1)}, bf16[1024,16,64]{0,2,1:T(8,128)(2,1)}, u32[]{:S(2)}) copy-start(bf16[1024,16,64]{0,2,1:T(8,128)(2,1)} %copy-done.1) | copy-start | bytes 6291460 | tf_op jit(solution)/shard_map/while/body/eval_jaxpr/while
  878.5 15.2 copy-start.1
  966.1 11.9 copy-start
  978.0 7.9 copy-start.5
  985.9 41.6 %copy-start.2 = (bf16[1024,16,64]{0,2,1:T(8,128)(2,1)S(1)}, bf16[1024,16,64]{0,2,1:T(8,128)(2,1)}, u32[]{:S(2)}) copy-start(bf16[1024,16,64]{0,2,1:T(8,128)(2,1)} %copy-done.1) | copy-start | bytes 6291460 | tf_op jit(solution)/shard_map/while/body/eval_jaxpr/while
  1027.9 4.1 copy-start.10
  1027.9 4.1 copy-start.27
  1027.9 4.1 copy-start.30
  1027.9 4.1 copy-start.32
  1035.8 130.2 %reduce-scatter.8.cloned.1.call-start = ((), (), s32[]{:S(2)}) async-start(), calls=%async_computation.14 | async-start | bytes 2621440 | tf_op jit(solution)/shard_map/reduce_scatter | solution.py:291
  1035.8 6.8 copy-start.18
  1054.5 115.0 %reduce-scatter.10.cloned.1.call-start = ((), (), s32[]{:S(2)}) async-start(), calls=%async_computation.15 | async-start | bytes 2621440 | tf_op jit(solution)/shard_map/reduce_scatter | solution.py:291
  1066.0 249.5 %reduce-scatter.16.cloned.1.call-start = ((), (), s32[]{:S(2)}) async-start(), calls=%async_computation.18 | async-start | bytes 10485760 | tf_op jit(solution)/shard_map/reduce_scatter | solution.py:291
  1081.1 382.1 %reduce-scatter.18.cloned.1.call-start = ((), (), s32[]{:S(2)}) async-start(), calls=%async_computation.19 | async-start | bytes 10485760 | tf_op jit(solution)/shard_map/reduce_scatter | solution.py:291
  1095.9 514.7 %reduce-scatter.20.cloned.1.call-start = ((), (), s32[]{:S(2)}) async-start(), calls=%async_computation.20 | async-start | bytes 10485760 | tf_op jit(solution)/shard_map/reduce_scatter | solution.py:291
  1150.1 5.4 copy-start.36
  1150.1 5.4 copy-start.37
  (21 other events, 46.2 us)
Sparse Core Ops, SparseCore 0:
  9.6 48.7 all-gather.11
  60.0 44.7 all-gather.13
  106.4 44.6 all-gather.15
  152.5 44.7 all-gather.17
  198.7 148.3 all-gather.21
  348.5 147.8 all-gather.19
  498.0 147.8 all-gather.23
  713.2 42.0 reduce-scatter.13
  1035.9 42.0 reduce-scatter.11
  1080.2 43.1 reduce-scatter.7
  1125.8 43.6 reduce-scatter.9
  1171.7 143.7 reduce-scatter.15
  1317.9 145.1 reduce-scatter.17
  1465.4 145.1 reduce-scatter.19
where the time goes:
time: 1960 us; the launch traced here: 1950 us
  waiting for transfers between devices  841 us (43%)
  matrix products  419 us (21%)
  blocking collectives  379 us (19%)
  local copies, waits for them, and re-layouts  161 us (8%)
  other arithmetic  131 us (7%)
    reduce_scatter x7, waiting for transfers between devices, shards(): lax.psum_scatter(for_sending((grad_gain_one, grad_bias_one, grad_query, g...  445 us
    psum x1, blocking collectives, shards(): weight_done = tuple(lax.psum(tuple(all_parts), 'wide'))  330 us
    all_gather x1, waiting for transfers between devices, shards(): lax.all_gather(w_gate, 'narrow', axis=0, tiled=True)  133 us
    all_gather x1, waiting for transfers between devices, shards(): lax.all_gather(w_down, 'narrow', axis=0, tiled=True)  133 us
    dynamic_update_slice x4, local copies, waits for them, and re-layouts, attend_row(): lax.map(one_block, (split_blocks(queries_row), split_blocks(segment_row)))  83.3 us
    all_gather x1, waiting for transfers between devices, shards(): lax.all_gather(w_up, 'narrow', axis=0, tiled=True)  79.9 us
    dot_general x4, matrix products, masked_scores(): jnp.einsum('qhe,khe->hqk', query_block, keys_row, preferred_element_type=...  60.7 us
    convert_element_type x2, other arithmetic, one_block(): grad_scores = (probability * (grad_probs - row_dot)).astype(jnp.bfloat16)  55.5 us
  transfers between devices with their start and end apart: 14, of which 9 were waited for; matrix products, arithmetic and copies ran while one was open for 32% of the time, Pallas kernels for 0%

commit v1 on v0

--- a/solution.py
+++ b/solution.py
@@ -13,12 +13,10 @@
 masked_score = -1e30
 
 
-def for_sending(shard):
-    return jax.tree.map(lambda a: a.astype(jnp.bfloat16) if a.dtype == jnp.float32 else a, shard)
-
-
 def segments_positions(lengths, row_len):
-    ends = jnp.cumsum(lengths, axis=-1)
+    order = jnp.arange(lengths.shape[-1], dtype=jnp.int32)
+    before = order[:, None] <= order[None, :]
+    ends = jnp.sum(jnp.where(before[None], lengths[:, :, None], 0), axis=1)
     starts = ends - lengths
     places = jnp.arange(row_len, dtype=jnp.int32)
     inside = (places[None, :, None] >= starts[:, None, :]) & (
@@ -162,21 +160,22 @@
     rows_here, row_len, features = tokens.shape
     heads_count = features // HEAD
     head_shape = (rows_here, row_len, heads_count, HEAD)
-    gain_one, bias_one, query_full, key_full, value_full, out_full = (
-        lax.all_gather(ln1_gain, "narrow", axis=0, tiled=True),
-        lax.all_gather(ln1_bias, "narrow", axis=0, tiled=True),
-        lax.all_gather(w_query, "narrow", axis=0, tiled=True),
-        lax.all_gather(w_key, "narrow", axis=0, tiled=True),
-        lax.all_gather(w_value, "narrow", axis=0, tiled=True),
-        lax.all_gather(w_out, "narrow", axis=0, tiled=True),
-    )
-    gain_two, bias_two, gate_full, up_full, down_full = (
-        lax.all_gather(ln2_gain, "narrow", axis=0, tiled=True),
-        lax.all_gather(ln2_bias, "narrow", axis=0, tiled=True),
-        lax.all_gather(w_gate, "narrow", axis=0, tiled=True),
-        lax.all_gather(w_up, "narrow", axis=0, tiled=True),
-        lax.all_gather(w_down, "narrow", axis=0, tiled=True),
-    )
+    wide_place = lax.axis_index("wide")
+    wide_size = lax.axis_size("wide")
+
+    def gather_whole(shard):
+        share = shard.shape[0] // wide_size
+        piece = lax.dynamic_slice_in_dim(shard, wide_place * share, share, axis=0)
+        return lax.all_gather(piece, ("narrow", "wide"), axis=0, tiled=True)
+
+    vectors = lax.all_gather(
+        jnp.stack([ln1_gain, ln1_bias, ln2_gain, ln2_bias]), "narrow", axis=1, tiled=True
+    )
+    gain_one, bias_one, gain_two, bias_two = vectors[0], vectors[1], vectors[2], vectors[3]
+    attn_full = gather_whole(jnp.concatenate([w_query, w_key, w_value, w_out], axis=1))
+    query_full, key_full, value_full, out_full = jnp.split(attn_full, 4, axis=1)
+    gate_full, up_full = jnp.split(gather_whole(jnp.concatenate([w_gate, w_up], axis=1)), 2, axis=1)
+    down_full = gather_whole(w_down)
     segment, position = segments_positions(lengths, row_len)
     cos_table, sin_table = rotary_tables(position, HEAD)
     tokens_flat = tokens.reshape(rows_here * row_len, features).astype(jnp.float32)
@@ -209,13 +208,6 @@
     hidden = (silu_gate * up_pre).astype(jnp.bfloat16)
     final = mixed + jnp.dot(hidden, down_full, preferred_element_type=jnp.float32)
     output = final.astype(jnp.bfloat16).reshape(tokens.shape)
-    gain_two, bias_two, gate_full, up_full, down_full = (
-        lax.all_gather(ln2_gain, "narrow", axis=0, tiled=True),
-        lax.all_gather(ln2_bias, "narrow", axis=0, tiled=True),
-        lax.all_gather(w_gate, "narrow", axis=0, tiled=True),
-        lax.all_gather(w_up, "narrow", axis=0, tiled=True),
-        lax.all_gather(w_down, "narrow", axis=0, tiled=True),
-    )
     cotangent_flat = cotangent.reshape(rows_here * row_len, features)
     grad_down = jnp.einsum("tf,td->fd", hidden, cotangent_flat, preferred_element_type=jnp.float32)
     grad_hidden = jnp.einsum(
@@ -240,14 +232,16 @@
     grad_mixed = cotangent_flat.astype(jnp.float32) + norm_back(
         grad_normed_two, hat_two, inverse_two, gain_two.astype(jnp.float32)
     )
-    ffn_grads = (grad_gain_two, grad_bias_two, grad_gate, grad_up, grad_down)
-    gain_one, bias_one, query_full, key_full, value_full, out_full = (
-        lax.all_gather(ln1_gain, "narrow", axis=0, tiled=True),
-        lax.all_gather(ln1_bias, "narrow", axis=0, tiled=True),
-        lax.all_gather(w_query, "narrow", axis=0, tiled=True),
-        lax.all_gather(w_key, "narrow", axis=0, tiled=True),
-        lax.all_gather(w_value, "narrow", axis=0, tiled=True),
-        lax.all_gather(w_out, "narrow", axis=0, tiled=True),
+
+    def sum_shards(grad):
+        piece = lax.psum_scatter(
+            grad.astype(jnp.bfloat16), ("narrow", "wide"), scatter_dimension=0, tiled=True
+        )
+        return lax.all_gather(piece, "wide", axis=0, tiled=True).astype(jnp.float32)
+
+    grad_down_sum = sum_shards(grad_down)
+    grad_gate_sum, grad_up_sum = jnp.split(
+        sum_shards(jnp.concatenate([grad_gate, grad_up], axis=1)), 2, axis=1
     )
     grad_res = grad_mixed.astype(jnp.bfloat16)
     grad_out = jnp.einsum("td,te->de", attended_low, grad_res, preferred_element_type=jnp.float32)
@@ -286,20 +280,27 @@
     input_grad = grad_mixed + norm_back(
         grad_normed_one, hat_one, inverse_one, gain_one.astype(jnp.float32)
     )
-    all_parts = jax.tree.map(
-        lambda part: part.astype(jnp.float32),
-        lax.psum_scatter(
-            for_sending(
-                (grad_gain_one, grad_bias_one, grad_query, grad_key, grad_value, grad_out)
-                + ffn_grads
-            ),
-            "narrow",
-            scatter_dimension=0,
-            tiled=True,
-        ),
-    )
-    weight_done = tuple(lax.psum(tuple(all_parts), "wide"))
-    return (output, input_grad.reshape(tokens.shape)) + weight_done
+    attn_sums = jnp.split(
+        sum_shards(jnp.concatenate([grad_query, grad_key, grad_value, grad_out], axis=1)), 4, axis=1
+    )
+    vector_sums = lax.psum(
+        jnp.stack([grad_gain_one, grad_bias_one, grad_gain_two, grad_bias_two]), ("wide", "narrow")
+    )
+    mine = lax.dynamic_slice_in_dim(
+        vector_sums, lax.axis_index("narrow") * ln1_gain.shape[0], ln1_gain.shape[0], axis=1
+    )
+    return (
+        output,
+        input_grad.reshape(tokens.shape),
+        mine[0],
+        mine[1],
+        *attn_sums,
+        mine[2],
+        mine[3],
+        grad_gate_sum,
+        grad_up_sum,
+        grad_down_sum,
+    )
 
 
 def solution(mesh):

time: 1960 us -> 1200 us (0.61)
  waiting for transfers between devices: 841 us -> 379 us
  blocking collectives: 379 us -> 56.2 us
  other arithmetic: 131 us -> 152 us
    all_gather x7 -> x6, waiting for transfers between devices: 392 us -> 82.3 us  [the longest x3 76.7 us: gather_whole(): return lax.all_gather(piece, ('narrow', 'wide'), axis=0, tiled=True)]
    psum x1, blocking collectives: 330 us -> 42.5 us  [shards(): lax.psum(jnp.stack([grad_gain_one, grad_bias_one, grad_gain_two, grad_bia...]
    reduce_scatter x7 -> x3, waiting for transfers between devices: 445 us -> 296 us  [sum_shards(): lax.psum_scatter(grad.astype(jnp.bfloat16), ('narrow', 'wide'), scatter_d...]
    all_gather x4 -> x1, blocking collectives: 38.8 us -> 13.7 us  [shards(): lax.all_gather(jnp.stack([ln1_gain, ln1_bias, ln2_gain, ln2_bias]), 'narr...]
    unnamed x94 -> x116, local copies, waits for them, and re-layouts: 38.7 us -> 46.5 us
  transfers between devices with their start and end apart: 14 -> 9, of which waited for: 9 -> 5; matrix products, arithmetic and copies ran while one was open for 32% -> 52% of each run, Pallas kernels for 0% -> 0%
where the time goes in v1:
time: 1200 us; the launch traced here: 1190 us
  matrix products  407 us (34%)
  waiting for transfers between devices  379 us (32%)
  local copies, waits for them, and re-layouts  176 us (15%)
  other arithmetic  152 us (13%)
  blocking collectives  56.2 us (5%)
  between operations  15 us (1%)
    reduce_scatter x3, waiting for transfers between devices, sum_shards(): lax.psum_scatter(grad.astype(jnp.bfloat16), ('narrow', 'wide'), scatter_d...  296 us
    dynamic_update_slice x4, local copies, waits for them, and re-layouts, attend_row(): lax.map(one_block, (split_blocks(queries_row), split_blocks(segment_row)))  83.3 us
    all_gather x3, waiting for transfers between devices, gather_whole(): return lax.all_gather(piece, ('narrow', 'wide'), axis=0, tiled=True)  76.7 us
    dot_general x4, matrix products, masked_scores(): jnp.einsum('qhe,khe->hqk', query_block, keys_row, preferred_element_type=...  59.9 us
    convert_element_type x2, other arithmetic, one_block(): grad_scores = (probability * (grad_probs - row_dot)).astype(jnp.bfloat16)  56.2 us
    dot_general x2, matrix products, one_block(): jnp.einsum('qhe,khe->hqk', grad_block, values_row, preferred_element_type...  51.9 us
    unnamed x116, local copies, waits for them, and re-layouts  46.5 us
    psum x1, blocking collectives, shards(): lax.psum(jnp.stack([grad_gain_one, grad_bias_one, grad_gain_two, grad_bia...  42.5 us
  transfers between devices with their start and end apart: 9, of which 5 were waited for; matrix products, arithmetic and copies ran while one was open for 52% of the time, Pallas kernels for 0%

profile of v1, /device:TPU:0, one launch (start us, length us, event | category | flops | bytes accessed | tf_op | source)
XLA Modules:
  0.0 1187.7 jit_solution(13804471004898187209)
XLA Ops:
  19.8 13.7 %all_gather.21 = bf16[4,1024]{1,0:T(4,128)(2,1)S(1)} all-gather(bf16[4,256]{1,0:T(4,128)(2,1)S(1)} %pad_maximum_fusion.6), channel_id=1, replica_groups=mesh['wide'=8,'narrow'=4] {'narrow'}, dimensions={1}, use_global_device_ids=true | all-gather | bytes 10240 | tf_op jit(solution)/shard_map/all_gather | solution.py:171
  40.1 51.7 %all-gather.7.cloned.1.call-done = bf16[1024,4096]{1,0:T(8,128)(2,1)} async-done(((bf16[32,4096]{1,0:T(8,128)(2,1)}), bf16[1024,4096]{1,0:T(8,128)(2,1)}) %all-gather.7.cloned.1.call-update) | async-done | bytes 8388624 | tf_op jit(solution)/shard_map/all_gather | solution.py:169
  91.8 6.2 fusion.91
  98.0 6.6 reshape.792
  117.6 6.1 fusion.66
  132.1 5.7 convolution_convert_fusion.8
  137.7 95.4 %while.47 = (s32[]{:T(128)}, bf16[2,512,16,64]{1,3,2,0:T(8,128)(2,1)}, f32[2,16,512]{2,1,0:T(8,128)S(1)}, s32[2,512]{1,0:T(2,128)S(1)}, s32[1024]{0:T(1024)S(1)}...) while((s32[]{:T(128)}, ...), condition=%wide.region_8.9_spmd, body=%wide.region_5.8_spmd.sunk | while | flops 2248663040 | bytes 135538864 | solution.py:94
  138.3 15.5 %fusion.159 = (f32[16,512]{1,0:T(8,128)S(1)}, f32[16,512,1024]{2,1,0:T(8,128)}) fusion(pred[512,1024]{1,0:T(8,128)(4,1)S(1)} %broadcast_compare_fusion.4, bf16[1024,16,64]{0,2,1:T(8,128)(2,1)S(1)} %get-tuple-element.564, bf16[2,512,16,64]{1,3,2,0:T(8,128)(2,1)} %get-tuple-element.563, s32[]{:T(128)S(6)} %copy.139), kind=kOutput, calls=%fused_computation.3.clone.1 | convolution fusion | flops 1098899456 | bytes 37257220 | tf_op jit(solution)/shard_map/while/body/eval_jaxpr/while/body/eval_jaxpr/qhe,khe->hqk/dot_general | solution.py:67
  153.8 15.5 %fusion.160 = f32[16,512]{1,0:T(8,128)S(1)} fusion(f32[16,512,1024]{2,1,0:T(8,128)} %get-tuple-element.525, f32[16,512]{1,0:T(8,128)S(1)} %get-tuple-element.526, pred[512,1024]{1,0:T(8,128)(4,1)S(1)} %broadcast_compare_fusion.4), kind=kLoop, calls=%fused_computation.4.clone.1 | loop fusion | flops 33546240 | bytes 34144256 | tf_op jit(solution)/shard_map/while/body/eval_jaxpr/while/body/eval_jaxpr/reduce_sum | solution.py:87
  169.3 14.8 %bitcast_dynamic-update-slice_fusion.4 = bf16[2,512,16,64]{1,3,2,0:T(8,128)(2,1)S(1)} fusion(bf16[2,512,16,64]{1,3,2,0:T(8,128)(2,1)S(1)} %copy-done.29, s32[]{:T(128)S(6)} %copy.139, bf16[1024,16,64]{0,2,1:T(8,128)(2,1)S(1)} %copy-done.5, f32[16,512,1024]{2,1,0:T(8,128)} %get-tuple-element.525, f32[16,512]{1,0:T(8,128)S(1)} %fusion.160, ...), kind=kOutput, calls=%fused_computation.6.clone.1 | convolution fusion | flops 1115684864 | bytes 38338564 | tf_op jit(solution)/shard_map/while/body/eval_jaxpr/while/body/eval_jaxpr/hqk,khe->qhe/dot_general | solution.py:89
  185.9 15.3 %fusion.159 = (f32[16,512]{1,0:T(8,128)S(1)}, f32[16,512,1024]{2,1,0:T(8,128)}) fusion(pred[512,1024]{1,0:T(8,128)(4,1)S(1)} %broadcast_compare_fusion.4, bf16[1024,16,64]{0,2,1:T(8,128)(2,1)S(1)} %get-tuple-element.564, bf16[2,512,16,64]{1,3,2,0:T(8,128)(2,1)} %get-tuple-element.563, s32[]{:T(128)S(6)} %copy.139), kind=kOutput, calls=%fused_computation.3.clone.1 | convolution fusion | flops 1098899456 | bytes 37257220 | tf_op jit(solution)/shard_map/while/body/eval_jaxpr/while/body/eval_jaxpr/qhe,khe->hqk/dot_general | solution.py:67
  201.2 15.8 %fusion.160 = f32[16,512]{1,0:T(8,128)S(1)} fusion(f32[16,512,1024]{2,1,0:T(8,128)} %get-tuple-element.525, f32[16,512]{1,0:T(8,128)S(1)} %get-tuple-element.526, pred[512,1024]{1,0:T(8,128)(4,1)S(1)} %broadcast_compare_fusion.4), kind=kLoop, calls=%fused_computation.4.clone.1 | loop fusion | flops 33546240 | bytes 34144256 | tf_op jit(solution)/shard_map/while/body/eval_jaxpr/while/body/eval_jaxpr/reduce_sum | solution.py:87
  217.0 14.6 %bitcast_dynamic-update-slice_fusion.4 = bf16[2,512,16,64]{1,3,2,0:T(8,128)(2,1)S(1)} fusion(bf16[2,512,16,64]{1,3,2,0:T(8,128)(2,1)S(1)} %copy-done.29, s32[]{:T(128)S(6)} %copy.139, bf16[1024,16,64]{0,2,1:T(8,128)(2,1)S(1)} %copy-done.5, f32[16,512,1024]{2,1,0:T(8,128)} %get-tuple-element.525, f32[16,512]{1,0:T(8,128)S(1)} %fusion.160, ...), kind=kOutput, calls=%fused_computation.6.clone.1 | convolution fusion | flops 1115684864 | bytes 38338564 | tf_op jit(solution)/shard_map/while/body/eval_jaxpr/while/body/eval_jaxpr/hqk,khe->qhe/dot_general | solution.py:89
  246.4 16.8 %fusion.79 = f32[4096,1024]{0,1:T(8,128)} fusion(bf16[4096,1024]{1,0:T(8,128)(2,1)} %all-gather.11.cloned.1.call-done, bf16[1,1024,1024]{2,1,0:T(8,128)(2,1)} %param.31), kind=kOutput, calls=%fused_computation.132 | convolution fusion | flops 8589934592 | bytes 27262976 | tf_op jit(solution)/shard_map/td,fd->tf/dot_general | solution.py:213
  263.2 25.0 %all-gather.9.cloned.1.call-done = bf16[1024,8192]{1,0:T(8,128)(2,1)} async-done(((bf16[32,8192]{1,0:T(8,128)(2,1)}), bf16[1024,8192]{1,0:T(8,128)(2,1)}) %all-gather.9.cloned.1.call-update) | async-done | bytes 16777232 | tf_op jit(solution)/shard_map/all_gather | solution.py:169
  288.2 15.1 %fusion.42 = f32[1024,4096]{1,0:T(8,128)} fusion(bf16[1024,1024]{0,1:T(8,128)(2,1)S(1)} %add_convert_fusion.2, bf16[1024,8192]{1,0:T(8,128)(2,1)} %all-gather.9.cloned.1.call-done), kind=kOutput, calls=%fused_computation.64 | convolution fusion | flops 8589934592 | bytes 27262976 | tf_op jit(solution)/shard_map/dot_general | solution.py:204
  303.3 28.0 %fusion.33 = (bf16[1024,4096]{1,0:T(8,128)(2,1)}, bf16[1024,4096]{1,0:T(8,128)(2,1)}, bf16[1024,4096]{1,0:T(8,128)(2,1)}) fusion(f32[4096,1024]{0,1:T(8,128)} %fusion.79, f32[1024,4096]{1,0:T(8,128)} %fusion.42, bf16[1024,1024]{0,1:T(8,128)(2,1)S(1)} %add_convert_fusion.2, bf16[1024,8192]{1,0:T(8,128)(2,1)} %all-gather.9.cloned.1.call-done), kind=kOutput, calls=%fused_computation.49 | convolution fusion | flops 8652849152 | bytes 69206016 | tf_op jit(solution)/shard_map/dot_general | solution.py:205
  331.3 12.8 %fusion.36 = f32[1024,1024]{0,1:T(8,128)S(1)} fusion(bf16[1024,4096]{1,0:T(8,128)(2,1)} %get-tuple-element.380, bf16[1024,8192]{1,0:T(8,128)(2,1)} %all-gather.9.cloned.1.call-done), kind=kOutput, calls=%fused_computation.58 | convolution fusion | flops 8589934592 | bytes 20971520 | tf_op jit(solution)/shard_map/tf,df->td/dot_general | solution.py:227
  344.2 15.9 %multiply_reduce_fusion.1 = (f32[1024]{0:T(1024)}, f32[1024]{0:T(1024)S(1)}, f32[1024]{0:T(1024)S(1)}, f32[1024]{0:T(1024)}, f32[1024,1024]{0,1:T(8,128)S(1)}) fusion(f32[1024,1024]{0,1:T(8,128)S(1)} %copy-done.7, f32[1024]{0:T(1024)S(1)} %add_rsqrt_fusion, f32[1024]{0:T(1024)S(1)} %broadcast_multiply_fusion.7, f32[1024]{0:T(1024)S(1)} %bitcast.253, ...), kind=kOutput, calls=%fused_computation.105 | convolution fusion | flops 8600416256 | bytes 29388800 | tf_op jit(solution)/shard_map/tf,df->td/dot_general | solution.py:224
  371.5 5.6 copy.95
  377.1 14.6 %convolution_convert_fusion = bf16[4096,1024]{1,0:T(8,128)(2,1)} fusion(bf16[1024,4096]{1,0:T(8,128)(2,1)} %get-tuple-element.381, bf16[1,1024,1024]{2,1,0:T(8,128)(2,1)S(1)} %copy-done.26), kind=kOutput, calls=%fused_computation.55 | convolution fusion | flops 8594128896 | bytes 18874368 | tf_op jit(solution)/shard_map/tf,td->fd/dot_general | solution.py:212
  393.3 299.3 %while.48 = (s32[]{:T(128)}, f32[1024,16,64]{0,2,1:T(8,128)}, f32[1024,16,64]{0,2,1:T(8,128)}, f32[2,512,16,64]{1,0,3,2:T(2,128)}, bf16[2,512,16,64]{1,3,2,0:T(8...) while((s32[]{:T(128)}, f32[1024,16,64]{0,2,1:T(8,128)}, ...), condition=%wide.region_15.16_spmd.clone, body=%wide.region_13.15_spmd.clone.sunk | while | flops 5500821504 | bytes 300132512 | solution.py:138
  394.1 14.6 %fusion.170 = f32[16,512,1024]{2,1,0:T(8,128)} fusion(bf16[1024,16,64]{0,2,1:T(8,128)(2,1)S(1)} %get-tuple-element.600, bf16[2,512,16,64]{1,3,2,0:T(8,128)(2,1)} %get-tuple-element.597, s32[]{:T(128)S(6)} %copy.149), kind=kOutput, calls=%fused_computation.29.clone.1 | convolution fusion | flops 1073741824 | bytes 36700164 | tf_op jit(solution)/shard_map/while/body/eval_jaxpr/while/body/eval_jaxpr/qhe,khe->hqk/dot_general | solution.py:67
  408.8 17.8 %bitcast_add_fusion.6 = f32[1024,16,64]{0,2,1:T(8,128)} fusion(f32[1024,16,64]{0,2,1:T(8,128)} %get-tuple-element.582, f32[16,512,1024]{2,1,0:T(8,128)} %fusion.170, f32[16,512]{1,0:T(8,128)S(1)} %dynamic-slice_bitcast_fusion.2, pred[512,1024]{1,0:T(8,128)(4,1)S(1)} %broadcast_compare_fusion.5, pred[]{:T(512)S(6)} %compare.3, ...), kind=kOutput, calls=%fused_computation.22.clone.1 | convolution fusion | flops 1109393408 | bytes 43548676 | tf_op jit(solution)/shard_map/while/body/eval_jaxpr/while/body/eval_jaxpr/hqk,qhe->khe/dot_general | solution.py:123
  426.5 26.0 %multiply_reduce_fusion.7 = (f32[16,512]{1,0:T(8,128)S(1)}, f32[16,512,1024]{2,1,0:T(8,128)}) fusion(f32[16,512,1024]{2,1,0:T(8,128)} %fusion.170, f32[16,512]{1,0:T(8,128)S(1)} %dynamic-slice_bitcast_fusion.2, pred[512,1024]{1,0:T(8,128)(4,1)S(1)} %broadcast_compare_fusion.5, bf16[1024,16,64]{0,2,1:T(8,128)(2,1)} %get-tuple-element.603, ...), kind=kOutput, calls=%fused_computation.17.clone.1 | convolution fusion | flops 1115676672 | bytes 70844416 | tf_op jit(solution)/shard_map/while/body/eval_jaxpr/while/body/eval_jaxpr/qhe,khe->hqk/dot_general | solution.py:107
  452.5 28.4 %multiply_convert_fusion.3 = bf16[16,512,1024]{2,1,0:T(8,128)(2,1)} fusion(f32[16,512,1024]{2,1,0:T(8,128)} %get-tuple-element.538, f32[16,512,1024]{2,1,0:T(8,128)} %fusion.170, f32[16,512]{1,0:T(8,128)S(1)} %get-tuple-element.539, f32[16,512]{1,0:T(8,128)S(1)} %dynamic-slice_bitcast_fusion.2, pred[512,1024]{1,0:T(8,128)(4,1)S(1)} %broadcast_compare_fusion.5), kind=kLoop, calls=%fused_computation.16.clone.1 | loop fusion | flops 50331648 | bytes 84475904 | tf_op jit(solution)/shard_map/while/body/eval_jaxpr/while/body/eval_jaxpr/convert_element_type | solution.py:111
  480.9 8.9 multiply_bitcast_fusion.3
  489.8 11.1 bitcast_add_fusion.5
  504.4 38.1 %dynamic_update_slice.31 = f32[2,512,16,64]{1,0,3,2:T(2,128)} dynamic-update-slice(f32[2,512,16,64]{1,0,3,2:T(2,128)} %get-tuple-element.583, f32[1,512,16,64]{1,0,3,2:T(1,128)} %copy.132, s32[]{:T(128)S(6)} %copy.149, s32[]{:T(128)} %constant.104.clone.1..sunk, s32[]{:T(128)} %constant.104.clone.1..sunk, s32[]{:T(128)} %constant.104.clone.1..sunk) | dynamic-update-slice | bytes 4194308 | tf_op jit(solution)/shard_map/while/body/eval_jaxpr/while/body/jit(dynamic_update_index_in_dim)/dynamic_update_slice | solution.py:94
  542.9 14.4 %fusion.170 = f32[16,512,1024]{2,1,0:T(8,128)} fusion(bf16[1024,16,64]{0,2,1:T(8,128)(2,1)S(1)} %get-tuple-element.600, bf16[2,512,16,64]{1,3,2,0:T(8,128)(2,1)} %get-tuple-element.597, s32[]{:T(128)S(6)} %copy.149), kind=kOutput, calls=%fused_computation.29.clone.1 | convolution fusion | flops 1073741824 | bytes 36700164 | tf_op jit(solution)/shard_map/while/body/eval_jaxpr/while/body/eval_jaxpr/qhe,khe->hqk/dot_general | solution.py:67
  557.3 18.7 %bitcast_add_fusion.6 = f32[1024,16,64]{0,2,1:T(8,128)} fusion(f32[1024,16,64]{0,2,1:T(8,128)} %get-tuple-element.582, f32[16,512,1024]{2,1,0:T(8,128)} %fusion.170, f32[16,512]{1,0:T(8,128)S(1)} %dynamic-slice_bitcast_fusion.2, pred[512,1024]{1,0:T(8,128)(4,1)S(1)} %broadcast_compare_fusion.5, pred[]{:T(512)S(6)} %compare.3, ...), kind=kOutput, calls=%fused_computation.22.clone.1 | convolution fusion | flops 1109393408 | bytes 43548676 | tf_op jit(solution)/shard_map/while/body/eval_jaxpr/while/body/eval_jaxpr/hqk,qhe->khe/dot_general | solution.py:123
  576.1 25.9 %multiply_reduce_fusion.7 = (f32[16,512]{1,0:T(8,128)S(1)}, f32[16,512,1024]{2,1,0:T(8,128)}) fusion(f32[16,512,1024]{2,1,0:T(8,128)} %fusion.170, f32[16,512]{1,0:T(8,128)S(1)} %dynamic-slice_bitcast_fusion.2, pred[512,1024]{1,0:T(8,128)(4,1)S(1)} %broadcast_compare_fusion.5, bf16[1024,16,64]{0,2,1:T(8,128)(2,1)} %get-tuple-element.603, ...), kind=kOutput, calls=%fused_computation.17.clone.1 | convolution fusion | flops 1115676672 | bytes 70844416 | tf_op jit(solution)/shard_map/while/body/eval_jaxpr/while/body/eval_jaxpr/qhe,khe->hqk/dot_general | solution.py:107
  602.0 27.8 %multiply_convert_fusion.3 = bf16[16,512,1024]{2,1,0:T(8,128)(2,1)} fusion(f32[16,512,1024]{2,1,0:T(8,128)} %get-tuple-element.538, f32[16,512,1024]{2,1,0:T(8,128)} %fusion.170, f32[16,512]{1,0:T(8,128)S(1)} %get-tuple-element.539, f32[16,512]{1,0:T(8,128)S(1)} %dynamic-slice_bitcast_fusion.2, pred[512,1024]{1,0:T(8,128)(4,1)S(1)} %broadcast_compare_fusion.5), kind=kLoop, calls=%fused_computation.16.clone.1 | loop fusion | flops 50331648 | bytes 84475904 | tf_op jit(solution)/shard_map/while/body/eval_jaxpr/while/body/eval_jaxpr/convert_element_type | solution.py:111
  629.8 8.9 multiply_bitcast_fusion.3
  638.7 12.1 %bitcast_add_fusion.5 = f32[1024,16,64]{0,2,1:T(8,128)} fusion(f32[1024,16,64]{0,2,1:T(8,128)} %get-tuple-element.581, bf16[16,512,1024]{2,1,0:T(8,128)(2,1)} %multiply_convert_fusion.3, pred[]{:T(512)S(6)} %compare.3, bf16[2,512,16,64]{1,3,2,0:T(8,128)(2,1)S(1)} %copy-done.4, s32[]{:T(128)S(6)} %copy.149), kind=kOutput, calls=%fused_computation.23.clone.1 | convolution fusion | flops 1076887552 | bytes 26214404 | tf_op jit(solution)/shard_map/while/body/eval_jaxpr/while/body/eval_jaxpr/hqk,qhe->khe/dot_general | solution.py:118
  654.3 38.1 %dynamic_update_slice.31 = f32[2,512,16,64]{1,0,3,2:T(2,128)} dynamic-update-slice(f32[2,512,16,64]{1,0,3,2:T(2,128)} %get-tuple-element.583, f32[1,512,16,64]{1,0,3,2:T(1,128)} %copy.132, s32[]{:T(128)S(6)} %copy.149, s32[]{:T(128)} %constant.104.clone.1..sunk, s32[]{:T(128)} %constant.104.clone.1..sunk, s32[]{:T(128)} %constant.104.clone.1..sunk) | dynamic-update-slice | bytes 4194308 | tf_op jit(solution)/shard_map/while/body/eval_jaxpr/while/body/jit(dynamic_update_index_in_dim)/dynamic_update_slice | solution.py:94
  696.5 6.6 broadcast_in_dim.118
  734.1 11.3 copy.113
  745.5 12.9 %convolution_convert_fusion.2 = bf16[1024,4096]{1,0:T(8,128)(2,1)S(1)} fusion(bf16[1024,1024]{0,1:T(8,128)(2,1)} %copy-done.22, bf16[1024,4096]{1,0:T(8,128)(2,1)} %get-tuple-element.379), kind=kOutput, calls=%fused_computation.57 | convolution fusion | flops 8594128896 | bytes 18874368 | tf_op jit(solution)/shard_map/td,tf->df/dot_general | solution.py:220
  758.4 11.3 convolution_convert_fusion.1
  769.7 6.9 pad_maximum_fusion
  777.4 115.5 %reduce-scatter.10.cloned.1.call-done = bf16[32,4096]{1,0:T(8,128)(2,1)} async-done(((bf16[1024,4096]{1,0:T(8,128)(2,1)}), bf16[32,4096]{1,0:T(8,128)(2,1)}) %reduce-scatter.10.cloned.1.call-update) | async-done | bytes 262160 | tf_op jit(solution)/shard_map/reduce_scatter | solution.py:237
  892.9 180.8 %reduce-scatter.6.cloned.1.call-done = bf16[32,8192]{1,0:T(8,128)(2,1)} async-done(((bf16[1024,8192]{1,0:T(8,128)(2,1)}), bf16[32,8192]{1,0:T(8,128)(2,1)}) %reduce-scatter.6.cloned.1.call-update) | async-done | bytes 524304 | tf_op jit(solution)/shard_map/reduce_scatter | solution.py:237
  1073.8 15.3 %fusion.74 = bf16[1,1024,1024]{1,2,0:T(8,128)(2,1)} fusion(f32[1024,1024]{0,1:T(8,128)} %copy-done.6, bf16[1024,4096]{1,0:T(8,128)(2,1)} %get-tuple-element.381, bf16[4096,1024]{1,0:T(8,128)(2,1)} %all-gather.11.cloned.1.call-done), kind=kOutput, calls=%fused_computation.117 | convolution fusion | flops 8592031744 | bytes 23068672 | tf_op jit(solution)/shard_map/dot_general | solution.py:209
  1112.1 5.4 copy.103
  1117.6 42.5 %psum.7 = f32[4,1024]{1,0:T(4,128)S(1)} all-reduce(f32[4,1024]{1,0:T(4,128)S(1)} %pad_maximum_fusion.5), channel_id=1, replica_groups=mesh['wide'=8,'narrow'=4] {'wide','narrow'}, use_global_device_ids=true, to_apply=%region_22.23 | all-reduce | flops 4096 | bytes 32768 | tf_op jit(solution)/shard_map/psum | solution.py:286
  1168.5 5.6 all-gather.15.cloned.1.call-done
  1174.1 6.8 fusion.111
  (236 shorter events, 144.3 us)
Async XLA Ops:
  7.2 84.6 %all-gather.7.cloned.1.call-start = ((), (), s32[]{:S(2)}) async-start(), calls=%async_computation.3 | async-start | bytes 8650752 | tf_op jit(solution)/shard_map/all_gather | solution.py:169
  7.3 4.7 copy-start.51
  7.3 4.7 copy-start.52
  7.3 4.7 copy-start.53
  7.3 4.7 copy-start.54
  7.3 4.8 copy-start.55
  9.1 237.3 %all-gather.11.cloned.1.call-start = ((), (), s32[]{:S(2)}) async-start(), calls=%async_computation.5 | async-start | bytes 8650752 | tf_op jit(solution)/shard_map/all_gather | solution.py:169
  9.9 278.3 %all-gather.9.cloned.1.call-start = ((), (), s32[]{:S(2)}) async-start(), calls=%async_computation.4 | async-start | bytes 17301504 | tf_op jit(solution)/shard_map/all_gather | solution.py:169
  11.9 764.8 %reduce-scatter.8.cloned.1.call-start = ((), (), s32[]{:S(2)}) async-start(), calls=%async_computation.9 | async-start | bytes 8650752 | tf_op jit(solution)/shard_map/reduce_scatter | solution.py:237
  15.1 110.3 %copy-start.9 = (bf16[1,1024,1024]{1,2,0:T(8,128)(2,1)}, bf16[1,1024,1024]{1,2,0:T(8,128)(2,1)S(1)}, u32[]{:S(2)}) copy-start(bf16[1,1024,1024]{1,2,0:T(8,128)(2,1)S(1)} %copy.85) | copy-start | bytes 6291460
  34.5 95.9 %copy-start.18 = (f32[1024,64]{0,1:T(8,128)}, f32[1024,64]{0,1:T(8,128)S(1)}, u32[]{:S(2)}) copy-start(f32[1024,64]{0,1:T(8,128)S(1)} %get-tuple-element.398) | copy-start | bytes 786436
  34.5 95.9 %copy-start.20 = (f32[1024,64]{0,1:T(8,128)}, f32[1024,64]{0,1:T(8,128)S(1)}, u32[]{:S(2)}) copy-start(f32[1024,64]{0,1:T(8,128)S(1)} %get-tuple-element.399) | copy-start | bytes 786436
  38.8 92.9 %copy-start.39 = (f32[1024]{0:T(1024)}, f32[1024]{0:T(1024)S(1)}, u32[]{:S(2)}) copy-start(f32[1024]{0:T(1024)S(1)} %broadcast_multiply_fusion.8) | copy-start | bytes 12292
  39.4 92.2 %copy-start.42 = (f32[1024]{0:T(1024)}, f32[1024]{0:T(1024)S(1)}, u32[]{:S(2)}) copy-start(f32[1024]{0:T(1024)S(1)} %add_rsqrt_fusion.1) | copy-start | bytes 12292
  40.0 91.6 %copy-start.44 = (f32[1,1024]{1,0:T(1,128)}, f32[1,1024]{1,0:T(1,128)S(1)}, u32[]{:S(2)}) copy-start(f32[1,1024]{1,0:T(1,128)S(1)} %get-tuple-element.409) | copy-start | bytes 12292
  40.0 91.6 %copy-start.49 = (f32[1,1024]{1,0:T(1,128)}, f32[1,1024]{1,0:T(1,128)S(1)}, u32[]{:S(2)}) copy-start(f32[1,1024]{1,0:T(1,128)S(1)} %get-tuple-element.408) | copy-start | bytes 12292
  153.8 15.5 %copy-start.5 = (bf16[1024,16,64]{0,2,1:T(8,128)(2,1)S(1)}, bf16[1024,16,64]{0,2,1:T(8,128)(2,1)}, u32[]{:S(2)}) copy-start(bf16[1024,16,64]{0,2,1:T(8,128)(2,1)} %get-tuple-element.565) | copy-start | bytes 6291460 | tf_op jit(solution)/shard_map/while/body/eval_jaxpr/while
  153.8 15.6 %copy-start.29 = (bf16[2,512,16,64]{1,3,2,0:T(8,128)(2,1)S(1)}, bf16[2,512,16,64]{1,3,2,0:T(8,128)(2,1)}, u32[]{:S(2)}) copy-start(bf16[2,512,16,64]{1,3,2,0:T(8,128)(2,1)} %get-tuple-element.550) | copy-start | bytes 6291460 | tf_op jit(solution)/shard_map/while/body/eval_jaxpr/while
  201.2 15.8 %copy-start.5 = (bf16[1024,16,64]{0,2,1:T(8,128)(2,1)S(1)}, bf16[1024,16,64]{0,2,1:T(8,128)(2,1)}, u32[]{:S(2)}) copy-start(bf16[1024,16,64]{0,2,1:T(8,128)(2,1)} %get-tuple-element.565) | copy-start | bytes 6291460 | tf_op jit(solution)/shard_map/while/body/eval_jaxpr/while
  201.2 15.8 %copy-start.29 = (bf16[2,512,16,64]{1,3,2,0:T(8,128)(2,1)S(1)}, bf16[2,512,16,64]{1,3,2,0:T(8,128)(2,1)}, u32[]{:S(2)}) copy-start(bf16[2,512,16,64]{1,3,2,0:T(8,128)(2,1)} %get-tuple-element.550) | copy-start | bytes 6291460 | tf_op jit(solution)/shard_map/while/body/eval_jaxpr/while
  233.2 5.6 copy-start.2
  233.2 5.6 copy-start.33
  233.2 5.6 copy-start.35
  233.2 5.6 copy-start.37
  233.2 5.6 copy-start.11
  238.8 4.9 copy-start.27
  246.4 57.0 %copy-start.22 = (bf16[1024,1024]{0,1:T(8,128)(2,1)}, bf16[1024,1024]{0,1:T(8,128)(2,1)S(1)}, u32[]{:S(2)}) copy-start(bf16[1024,1024]{0,1:T(8,128)(2,1)S(1)} %add_convert_fusion.2) | copy-start | bytes 6291460
  331.3 12.8 %copy-start.7 = (f32[1024,1024]{0,1:T(8,128)S(1)}, f32[1024,1024]{0,1:T(8,128)}, u32[]{:S(2)}) copy-start(f32[1024,1024]{0,1:T(8,128)} %copy-done.6) | copy-start | bytes 12582916
  344.2 16.0 %copy-start.17 = (bf16[1,1024,1024]{1,2,0:T(8,128)(2,1)S(1)}, bf16[1,1024,1024]{1,2,0:T(8,128)(2,1)}, u32[]{:S(2)}) copy-start(bf16[1,1024,1024]{1,2,0:T(8,128)(2,1)} %copy.89) | copy-start | bytes 6291460
  371.5 5.6 copy-start.26
  391.7 501.1 %reduce-scatter.10.cloned.1.call-start = ((), (), s32[]{:S(2)}) async-start(), calls=%async_computation.11 | async-start | bytes 8650752 | tf_op jit(solution)/shard_map/reduce_scatter | solution.py:237
  480.9 8.9 copy-start.4
  629.8 8.9 copy-start.4
  696.5 6.7 copy-start.21
  714.2 12.7 %copy-start.31 = (bf16[1024,16,64]{0,2,1:T(8,128)(2,1)}, bf16[1024,16,64]{0,2,1:T(8,128)(2,1)S(1)}, u32[]{:S(2)}) copy-start(bf16[1024,16,64]{0,2,1:T(8,128)(2,1)S(1)} %fusion.69) | copy-start | bytes 6291460
  714.2 4.5 copy-start.14
  714.2 5.1 copy-start.28
  745.4 328.3 %reduce-scatter.6.cloned.1.call-start = ((), (), s32[]{:S(2)}) async-start(), calls=%async_computation.7 | async-start | bytes 17301504 | tf_op jit(solution)/shard_map/reduce_scatter | solution.py:237
  745.5 12.9 %copy-start.23 = (bf16[1024,1024]{0,1:T(8,128)(2,1)S(1)}, bf16[1024,1024]{0,1:T(8,128)(2,1)}, u32[]{:S(2)}) copy-start(bf16[1024,1024]{0,1:T(8,128)(2,1)} %copy-done.22) | copy-start | bytes 6291460
  776.6 384.1 %all-gather.17.cloned.1.call-start = ((), (), s32[]{:S(2)}) async-start(), calls=%async_computation.10 | async-start | bytes 2359296 | tf_op jit(solution)/shard_map/all_gather | solution.py:240
  777.4 387.4 %all-gather.13.cloned.1.call-start = ((), (), s32[]{:S(2)}) async-start(), calls=%async_computation.6 | async-start | bytes 2359296 | tf_op jit(solution)/shard_map/all_gather | solution.py:240
  892.9 281.2 %all-gather.15.cloned.1.call-start = ((), (), s32[]{:S(2)}) async-start(), calls=%async_computation.8 | async-start | bytes 4718592 | tf_op jit(solution)/shard_map/all_gather | solution.py:240
  1093.2 3.8 copy-start.16
  1097.0 5.8 slice-start
  1098.6 4.2 slice-start.1
  1112.1 5.4 copy-start.47
  1112.1 5.4 copy-start.48
  1174.1 6.9 copy-start.1
  (23 other events, 47.3 us)
Sparse Core Ops, SparseCore 0:
  11.5 80.2 all-gather.6
  95.2 76.0 all-gather.10
  174.7 113.4 all-gather.8
  391.9 146.6 reduce-scatter.7
  745.5 147.2 reduce-scatter.9
  895.0 178.6 reduce-scatter.5
  1075.6 29.6 all-gather.16
  1107.2 27.9 all-gather.12
  1137.1 36.9 all-gather.14

commit v2 on v1

v2 whole, which is shorter than its diff:
```python
import functools
import math

import jax
import jax.numpy as jnp
import numpy as np
from jax import lax
from jax.experimental import pallas as pl
from jax.experimental.pallas import tpu as pltpu
from jax.sharding import PartitionSpec as P

F32 = jnp.float32
BF = jnp.bfloat16
HEAD = 64
BLK = 256
LOG2E = 1.4426950408889634
EPS = 1e-5
ROTARY_BASE = 10000.0
ANY = pl.BlockSpec(memory_space=pl.ANY)
MIB = 1024 * 1024
ZN = 4


def nn(a, b):
    return lax.dot_general(a, b, (((1,), (0,)), ((), ())), preferred_element_type=F32)


def nt(a, b):
    return lax.dot_general(a, b, (((1,), (1,)), ((), ())), preferred_element_type=F32)


def tn(a, b):
    return lax.dot_general(a, b, (((0,), (0,)), ((), ())), preferred_element_type=F32)


def lanes(shape):
    return lax.broadcasted_iota(jnp.int32, shape, len(shape) - 1)


def hat_of(x):
    center = x - jnp.mean(x, axis=-1, keepdims=True)
    rstd = lax.rsqrt(jnp.mean(center * center, axis=-1, keepdims=True) + EPS)
    return center * rstd, rstd


def norm_back(grad, hat, rstd, gain):
    scaled = grad * gain
    first = jnp.mean(scaled, axis=-1, keepdims=True)
    second = jnp.mean(scaled * hat, axis=-1, keepdims=True)
    return rstd * (scaled - first - hat * second)


def halves(u):
    first = lax.rem(lanes(u.shape), HEAD) < HEAD // 2
    ahead = pltpu.roll(u, u.shape[-1] - HEAD // 2, axis=u.ndim - 1)
    behind = pltpu.roll(u, HEAD // 2, axis=u.ndim - 1)
    return jnp.where(first, ahead, behind)


def turn(u, cos, sin_signed):
    return u * cos + halves(u) * sin_signed


def unturn(g, cos, sin_signed):
    return g * cos - halves(g) * sin_signed


def copies(pairs, sems):
    made = [pltpu.make_async_copy(a, b, sems.at[i]) for i, (a, b) in enumerate(pairs)]
    for one in made:
        one.start()
    return made


def split_three(v):
    top = v.astype(BF).astype(F32)
    rest = v - top
    mid = rest.astype(BF).astype(F32)
    return top, mid, rest - mid


MESH_ID = pl.DeviceIdType.MESH


def place():
    w, z = lax.axis_index("wide"), lax.axis_index("narrow")
    c, a, b = lax.rem(w, 2), lax.rem(w // 2, 2), lax.rem(w // 4, 2)
    return dict(w=w, z=z, c=c, a=a, b=b, wc=w + 1 - 2 * c, wx=w + 2 - 4 * a, wy=w + 4 - 8 * b)


def around(me, k):
    return lax.rem(me["z"] + k + ZN, ZN)


def remote(src, dst, ssem, rsem, w, z):
    return pltpu.make_async_remote_copy(
        src_ref=src, dst_ref=dst, send_sem=ssem, recv_sem=rsem, device_id=(w, z), device_id_type=MESH_ID
    )


def meet(me):
    barrier = pltpu.get_barrier_semaphore()
    others = [(me["wc"], me["z"]), (me["wx"], me["z"]), (me["wy"], me["z"])]
    others += [(me["w"], around(me, k)) for k in range(1, ZN)]
    for other in others:
        pl.semaphore_signal(barrier, inc=1, device_id=other, device_id_type=MESH_ID)
    pl.semaphore_wait(barrier, len(others))


def part(start, size):
    return pl.ds(pl.multiple_of(start, size), size)


LEFT, RIGHT = pl.ds(0, 512), pl.ds(512, 512)


class Gather:
    def __init__(self, me, own, dst, ssem, rsem):
        self.me, self.own, self.dst, self.ssem, self.rsem = me, own, dst, ssem, rsem
        c, a, b = me["c"], me["a"], me["b"]
        self.mine = part(c * 128 + a * 64 + b * 32, 32)
        self.from_x = part(c * 128 + (1 - a) * 64 + b * 32, 32)
        self.from_y = part(c * 128 + a * 64 + (1 - b) * 32, 32)
        self.core_half = part(c * 128, 128)

    def along(self, p, k, rows, cols, at, w, z, owner):
        ref = self.dst.at[p, owner, rows, cols]
        return remote(ref, ref, self.ssem.at[p, at + k - 1], self.rsem.at[p, at + k - 1], w, z)

    def z_copy(self, p, k):
        me = self.me
        src, dst = self.own.at[p, self.mine], self.dst.at[p, me["z"], self.mine]
        return remote(src, dst, self.ssem.at[p, k - 1], self.rsem.at[p, k - 1], me["w"], around(me, k))

    def x_copy(self, p, k):
        return self.along(p, k, self.mine, pl.ds(0, 1024), 3, self.me["wx"], self.me["z"], around(self.me, -k))

    def y_copy(self, p, k):
        return self.along(p, k, self.mine, pl.ds(0, 1024), 6, self.me["wy"], self.me["z"], around(self.me, -k))

    def xy_copy(self, p, k):
        return self.along(p, k, self.from_y, LEFT, 9, self.me["wx"], self.me["z"], around(self.me, -k))

    def yx_copy(self, p, k):
        return self.along(p, k, self.from_x, RIGHT, 12, self.me["wy"], self.me["z"], around(self.me, -k))

    def core_copy(self, p, k):
        return self.along(p, k, self.core_half, pl.ds(0, 1024), 15, self.me["wc"], self.me["z"], around(self.me, -k))

    def start_z(self, p):
        for k in range(1, ZN):
            self.z_copy(p, k).start()

    def stage_one(self, p):
        for k in range(1, ZN):
            self.z_copy(p, k).wait_recv()
            self.x_copy(p, k).start()
            self.y_copy(p, k).start()

    def stage_two(self, p):
        for k in range(1, ZN):
            self.y_copy(p, k).wait_recv()
            self.xy_copy(p, k).start()
            self.x_copy(p, k).wait_recv()
            self.yx_copy(p, k).start()

    def stage_core(self, p):
        for k in range(1, ZN):
            self.xy_copy(p, k).wait_recv()
            self.yx_copy(p, k).wait_recv()
            self.core_copy(p, k).start()

    def finish(self, p):
        for k in range(1, ZN):
            self.core_copy(p, k).wait_recv()
        for k in range(1, ZN):
            for copy in (self.z_copy, self.x_copy, self.y_copy, self.xy_copy, self.yx_copy, self.core_copy):
                copy(p, k).wait_send()


def add_up(*parts):
    total = parts[0].astype(F32)
    for one in parts[1:]:
        total = total + one.astype(F32)
    return total.astype(BF)


class Reduce:
    SCRATCH = [
        ((2, 4, 128, 1024), "r0"), ((4, 128, 1024), "s0"), ((2, 2, 4, 64, 512), "r1"), ((2, 4, 64, 512), "s1"),
        ((2, 2, 4, 32, 512), "r2"), ((4, 2, 32, 512), "s2"), ((2, 3, 2, 32, 512), "r3"), ((2, 2, 32, 512), "f"),
    ]

    def __init__(self, me, G, fin, bufs, ssem, rsem, lsem):
        self.me, self.G, self.fin, self.ssem, self.rsem, self.lsem = me, G, fin, ssem, rsem, lsem
        for (_shape, name), ref in zip(self.SCRATCH, bufs):
            setattr(self, name, ref)

    def to(self, p, i, src, dst, w, z=None):
        z = self.me["z"] if z is None else z
        slot = lax.rem(p, 2)
        return remote(src, dst, self.ssem.at[slot, i], self.rsem.at[slot, i], w, z)

    def copies(self, s, p):
        me = self.me
        a, b, c, slot = me["a"], me["b"], me["c"], lax.rem(p, 2)
        every = pl.ds(0, ZN)
        if s == 0:
            return [self.to(p, 0, self.G.at[slot, every, part((1 - c) * 128, 128)], self.r0.at[slot], me["wc"])]
        if s == 1:
            return [
                self.to(p, 1, self.s0.at[every, part((1 - a) * 64, 64), LEFT], self.r1.at[slot, 0], me["wx"]),
                self.to(p, 2, self.s0.at[every, part((1 - b) * 64, 64), RIGHT], self.r1.at[slot, 1], me["wy"]),
            ]
        if s == 2:
            return [
                self.to(p, 3, self.s1.at[0, every, part((1 - b) * 32, 32)], self.r2.at[slot, 0], me["wy"]),
                self.to(p, 4, self.s1.at[1, every, part((1 - a) * 32, 32)], self.r2.at[slot, 1], me["wx"]),
            ]
        if s == 3:
            return [
                self.to(p, 4 + k, self.s2.at[around(me, k)], self.r3.at[slot, k - 1], me["w"], around(me, k))
                for k in range(1, ZN)
            ]
        left = (part(c * 128 + a * 64 + b * 32, 32), LEFT)
        right = (part(c * 128 + b * 64 + a * 32, 32), RIGHT)
        if s == 4:
            return [
                self.to(p, 8, self.f.at[slot, 0], self.fin.at[p, left[0], left[1]], me["wy"]),
                self.to(p, 9, self.f.at[slot, 1], self.fin.at[p, right[0], right[1]], me["wx"]),
                pltpu.make_async_copy(self.f.at[slot, 0], self.fin.at[p, left[0], left[1]], self.lsem.at[slot, 0]),
                pltpu.make_async_copy(self.f.at[slot, 1], self.fin.at[p, right[0], right[1]], self.lsem.at[slot, 1]),
            ]
        if s == 5:
            left = self.fin.at[p, part(c * 128 + a * 64, 64), LEFT]
            right = self.fin.at[p, part(c * 128 + b * 64, 64), RIGHT]
            return [self.to(p, 10, left, left, me["wx"]), self.to(p, 11, right, right, me["wy"])]
        half = self.fin.at[p, part(c * 128, 128)]
        return [self.to(p, 12, half, half, me["wc"])]

    def start(self, s, p):
        for copy in self.copies(s, p):
            copy.start()

    def take(self, s, p):
        for copy in self.copies(s, p):
            copy.wait()
        me = self.me
        a, b, c, z, slot = me["a"], me["b"], me["c"], me["z"], lax.rem(p, 2)
        if s == 0:
            for k in range(ZN):
                self.s0[k] = add_up(self.G[slot, k, part(c * 128, 128), :], self.r0[slot, k])
        if s == 1:
            self.s1[0] = add_up(self.s0[:, part(a * 64, 64), 0:512], self.r1[slot, 0])
            self.s1[1] = add_up(self.s0[:, part(b * 64, 64), 512:1024], self.r1[slot, 1])
        if s == 2:
            self.s2[:, 0] = add_up(self.s1[0, :, part(b * 32, 32), :], self.r2[slot, 0])
            self.s2[:, 1] = add_up(self.s1[1, :, part(a * 32, 32), :], self.r2[slot, 1])
        if s == 3:
            self.f[slot] = add_up(self.s2[z], self.r3[slot, 0], self.r3[slot, 1], self.r3[slot, 2])

    def advance(self, s, p):
        self.take(s, p)
        if s < 6:
            self.start(s + 1, p)

    def slot(self, t, low, high):
        for s in range(6, -1, -1):
            p = t - 1 - s

            @pl.when((p >= low) & (p < high))
            def _due(s=s, p=p):
                self.advance(s, p)


def local_feed(gate, up, own, sems, i):
    at = 4 + 3 * (i // 2) + lax.rem(i, 2)
    made = []
    for j in range(ZN):
        cols = part(1024 * j + 128 * i, 128)
        made.append(pltpu.make_async_copy(gate.at[:, cols], own.at[at, :, pl.ds(128 * j, 128)], sems.at[1 + i, j]))
        to = pl.ds(512 + 128 * j, 128)
        made.append(pltpu.make_async_copy(up.at[:, cols], own.at[at, :, to], sems.at[1 + i, 4 + j]))
    return made


def local_down(down, own, sems, i):
    return pltpu.make_async_copy(down.at[part(256 * i, 256)], own.at[6 + 3 * i], sems.at[9, i])


def loop(n, body):
    def step(i, _):
        body(i)
        return 0

    lax.fori_loop(0, n, step, 0)


def starts(make):
    def body(i):
        made = make(i)
        for copy in made if isinstance(made, list) else [made]:
            copy.start()

    return body


def waits(make):
    def body(i):
        made = make(i)
        for copy in made if isinstance(made, list) else [made]:
            copy.wait()

    return body


def kernel_gather(q, k, v, o, gate, up, down, dst, own, lsem, ssem, rsem):
    me = place()
    z = me["z"]
    local = [pltpu.make_async_copy(m, own.at[i], lsem.at[0, i]) for i, m in enumerate((q, k, v, o))]
    for copy in local:
        copy.start()
    loop(8, starts(lambda i: local_feed(gate, up, own, lsem, i)))
    loop(4, starts(lambda i: local_down(down, own, lsem, i)))
    meet(me)
    g = Gather(me, own, dst, ssem, rsem)

    def put(p):
        return pltpu.make_async_copy(own.at[p], dst.at[p, z], lsem.at[10, p])

    for i, copy in enumerate(local):
        copy.wait()
        g.start_z(i)
    loop(8, waits(lambda i: local_feed(gate, up, own, lsem, i)))
    loop(4, waits(lambda i: local_down(down, own, lsem, i)))
    n = dst.shape[0]
    loop(n, starts(put))

    def slot(t, _):
        for stage, lag in ((g.finish, 4), (g.stage_core, 3), (g.stage_two, 2), (g.stage_one, 1)):
            p = t - lag

            @pl.when((p >= 0) & (p < n))
            def _due(stage=stage, p=p):
                stage(p)

        @pl.when((t >= 4) & (t < n))
        def _z():
            g.start_z(t)

        return 0

    lax.fori_loop(1, n + 4, slot, 0)
    loop(n, waits(put))


def run_gather(*shards_):
    return pl.pallas_call(
        kernel_gather,
        name="weights",
        out_shape=jax.ShapeDtypeStruct((16, ZN, 256, 1024), BF),
        in_specs=[ANY] * 7,
        out_specs=ANY,
        scratch_shapes=[
            pltpu.VMEM((16, 256, 1024), BF),
            pltpu.SemaphoreType.DMA((11, 16)), pltpu.SemaphoreType.DMA((16, 18)), pltpu.SemaphoreType.DMA((16, 18)),
        ],
        compiler_params=pltpu.CompilerParams(collective_id=0, has_side_effects=True, vmem_limit_bytes=40 * MIB),
    )(*shards_)


def kernel_reduce(Ga_h, G_h, fin, G, *rest):
    bufs, (ssem, rsem, lsem, gsem) = rest[:8], rest[8:]
    me = place()
    n = G_h.shape[0]

    def load(p):
        return pltpu.make_async_copy(G_h.at[p], G.at[lax.rem(p, 2)], gsem.at[lax.rem(p, 2)])

    def load_start(p):
        @pl.when(p < 4)
        def _attn():
            pltpu.make_async_copy(Ga_h.at[p], G.at[lax.rem(p, 2)], gsem.at[lax.rem(p, 2)]).start()

        @pl.when(p >= 4)
        def _feed():
            load(p).start()

    load_start(jnp.int32(0))
    meet(me)
    r = Reduce(me, G, fin, bufs, ssem, rsem, lsem)

    def slot(t, _):
        r.slot(t, 0, n)

        @pl.when(t < n)
        def _begin():
            load(t).wait()
            r.start(0, t)

        @pl.when(t + 1 < n)
        def _load():
            load_start(t + 1)

        return 0

    lax.fori_loop(0, n + 7, slot, 0)


def run_reduce(Ga, G):
    return pl.pallas_call(
        kernel_reduce,
        name="gradient_sums",
        out_shape=jax.ShapeDtypeStruct((G.shape[0], 256, 1024), BF),
        in_specs=[ANY, ANY],
        out_specs=ANY,
        scratch_shapes=[pltpu.VMEM((2, ZN, 256, 1024), BF)]
        + [pltpu.VMEM(shape, BF) for shape, _ in Reduce.SCRATCH]
        + [
            pltpu.SemaphoreType.DMA((2, 13)), pltpu.SemaphoreType.DMA((2, 13)), pltpu.SemaphoreType.DMA((2, 2)),
            pltpu.SemaphoreType.DMA((2,)),
        ],
        compiler_params=pltpu.CompilerParams(collective_id=1, has_side_effects=True, vmem_limit_bytes=40 * MIB),
    )(Ga, G)


def attention_forward(i, pair, qaug, kaug, vaug, att):
    T = qaug.shape[0]
    low, high = max(0, i - 1) * BLK, min(T, (i + 2) * BLK)
    rows = slice(i * BLK, (i + 1) * BLK)
    outs, tops = [], []
    for one in range(2):
        cols = pl.ds(pl.multiple_of((2 * pair + one) * 128, 128), 128)
        scores = nt(qaug[rows, cols], kaug[low:high, cols])
        top = jnp.max(scores, axis=-1, keepdims=True)
        raised = jnp.exp2(scores - top).astype(BF)
        outs.append(nn(raised, vaug[low:high, cols]))
        tops.append(top)
    lane = lanes((BLK, 128))
    left = lane < HEAD
    for one in range(2):
        cols = pl.ds(pl.multiple_of((2 * pair + one) * 128, 128), 128)
        base = HEAD if one == 0 else 0
        parts = split_three(-(tops[one] + jnp.log2(outs[one])))
        kept = qaug[rows, cols].astype(F32)
        for k, part in enumerate(parts):
            kept = jnp.where(lane == base + 8 + k, part, kept)
        qaug[rows, cols] = kept.astype(BF)
    summed = pltpu.roll(jnp.where(left, outs[1], outs[0]), HEAD, axis=1)
    att[rows, pl.ds(pl.multiple_of(pair * 128, 128), 128)] = (
        jnp.where(left, outs[0], outs[1]) / summed
    ).astype(BF)


def project_turned(n1, W, cos, sin, aug, dest, scale):
    T = n1.shape[0]

    def block(j, _):
        flat = nn(n1[...], W[:, :, part(j * 256, 256)].reshape(n1.shape[1], 256))
        left = lanes((T, 128)) < HEAD
        for p in range(2):
            u = turn(flat[:, 128 * p : 128 * p + 128], cos[...], sin[...])
            if scale != 1.0:
                u = u * scale
            extra = aug[...].astype(F32)
            at = (4 * j + 2 * p) * 128
            dest[:, pl.ds(pl.multiple_of(at, 128), 128)] = jnp.where(left, u, extra).astype(BF)
            dest[:, pl.ds(pl.multiple_of(at + 128, 128), 128)] = jnp.where(left, extra, u).astype(BF)
        return 0

    lax.fori_loop(0, n1.shape[1] // 256, block, 0)


def project_values(n1, W, dest):
    T = n1.shape[0]

    def block(j, _):
        flat = nn(n1[...], W[:, :, part(j * 256, 256)].reshape(n1.shape[1], 256))
        left = lanes((T, 128)) < HEAD
        for p in range(2):
            u = flat[:, 128 * p : 128 * p + 128]
            at = (4 * j + 2 * p) * 128
            dest[:, pl.ds(pl.multiple_of(at, 128), 128)] = jnp.where(left, u, 1.0).astype(BF)
            dest[:, pl.ds(pl.multiple_of(at + 128, 128), 128)] = jnp.where(left, 1.0, u).astype(BF)
        return 0

    lax.fori_loop(0, n1.shape[1] // 256, block, 0)


def norm_rows(source, dest, gain, bias, n=BLK):
    def block(r, _):
        rows = pl.ds(pl.multiple_of(r * n, n), n)
        hat, _unused = hat_of(source[rows, :].astype(F32))
        dest[rows, :] = (hat * gain + bias).astype(BF)
        return 0

    lax.fori_loop(0, source.shape[0] // n, block, 0)


def kernel_a(
    tok_h, vec_h, cos_h, sin_h, aq_h, ak_h, W_h,
    mixed_h, n2_h, n1_h, att_h, qaug_h, kaug_h, vaug_h,
    x, vec, cos, sin, aq, ak, W, n1, qaug, kaug, vaug, att, mixed, sems, osems,
):
    T = x.shape[0]
    first = copies(
        [(tok_h, x), (vec_h, vec), (cos_h, cos), (sin_h, sin), (aq_h, aq), (ak_h, ak)]
        + [(W_h.at[k], W.at[k]) for k in range(4)],
        sems,
    )
    first[0].wait()
    first[1].wait()
    norm_rows(x, n1, vec[0:1, :], vec[1:2, :])
    for one in first[2:7]:
        one.wait()
    project_turned(n1, W.at[0], cos, sin, aq, qaug, LOG2E / math.sqrt(HEAD))
    first[7].wait()
    project_turned(n1, W.at[1], cos, sin, ak, kaug, 1.0)
    first[8].wait()
    project_values(n1, W.at[2], vaug)
    first[9].wait()
    outs = copies([(n1, n1_h), (kaug, kaug_h), (vaug, vaug_h)], osems)

    def per_pair(pair, _):
        for i in range(T // BLK):
            attention_forward(i, pair, qaug, kaug, vaug, att)
        return 0

    lax.fori_loop(0, x.shape[1] // 128, per_pair, 0)
    more = [pltpu.make_async_copy(qaug, qaug_h, osems.at[3]), pltpu.make_async_copy(att, att_h, osems.at[4])]
    for one in more:
        one.start()
    mixed[...] = x[...].astype(F32) + nn(att[...], W[3].reshape(x.shape[1], x.shape[1]))
    last = pltpu.make_async_copy(mixed, mixed_h, osems.at[5])
    last.start()
    outs[0].wait()
    norm_rows(mixed, n1, vec[2:3, :], vec[3:4, :])
    pltpu.make_async_copy(n1, n2_h, osems.at[6]).start()
    pltpu.make_async_copy(n1, n2_h, osems.at[6]).wait()
    for one in outs[1:] + more + [last]:
        one.wait()


def run_a(tok, vec, cos, sin, aq, ak, W):
    T, D = tok.shape
    sds = jax.ShapeDtypeStruct
    return pl.pallas_call(
        kernel_a,
        name="attention_forward",
        out_shape=[
            sds((T, D), F32), sds((T, D), BF), sds((T, D), BF), sds((T, D), BF),
            sds((T, 2 * D), BF), sds((T, 2 * D), BF), sds((T, 2 * D), BF),
        ],
        in_specs=[ANY] * 7,
        out_specs=[ANY] * 7,
        scratch_shapes=[
            pltpu.VMEM((T, D), BF), pltpu.VMEM(vec.shape, F32), pltpu.VMEM((T, 128), F32), pltpu.VMEM((T, 128), F32),
            pltpu.VMEM((T, 128), BF), pltpu.VMEM((T, 128), BF), pltpu.VMEM((4, ZN, D // ZN, D), BF), pltpu.VMEM((T, D), BF),
            pltpu.VMEM((T, 2 * D), BF), pltpu.VMEM((T, 2 * D), BF), pltpu.VMEM((T, 2 * D), BF),
            pltpu.VMEM((T, D), BF), pltpu.VMEM((T, D), F32),
            pltpu.SemaphoreType.DMA((10,)), pltpu.SemaphoreType.DMA((7,)),
        ],
        compiler_params=pltpu.CompilerParams(vmem_limit_bytes=60 * MIB),
    )(tok, vec, cos, sin, aq, ak, W)


def feed_chunk(n2, cot, gate_up, down, G, Gd, hid, dgu, oacc, gacc):
    D = n2.shape[1]
    half = hid.shape[1]
    gu = nn(n2[...], gate_up[...].reshape(D, 2 * half))
    g = gu[:, :half]
    u = gu[:, half:]
    gh = nt(cot[...], down[...].reshape(half, D))
    sig = 0.5 * jnp.tanh(0.5 * g) + 0.5
    silu = g * sig
    hid[...] = (silu * u).astype(BF)
    dgu[:, :half] = (gh * u * (sig + silu * (1.0 - sig))).astype(BF)
    dgu[:, half:] = (gh * silu).astype(BF)
    oacc[...] += nn(hid[...], down[...].reshape(half, D))
    gacc[...] += nt(dgu[...], gate_up[...].reshape(D, 2 * half))
    G[...] = tn(n2[...], dgu[...]).astype(BF).reshape(G.shape)
    Gd[...] = tn(hid[...], cot[...]).astype(BF).reshape(Gd.shape)


def kernel_b(
    n2_h, cot_h, mixed_h, vec_h, W_h,
    out_h, gm_h, vecs_h, G_h,
    n2, cot, mixed, vec, oacc, gacc, W, Wd, hid, dgu, G, Gd, vecs, s, sw, sg,
):
    T = n2.shape[0]
    chunks = 8
    first = copies([(n2_h, n2), (cot_h, cot), (mixed_h, oacc), (mixed_h, mixed), (vec_h, vec)], s)

    def wcp(c):
        at, slot = 4 + 3 * (c // 2), c % 2
        half = W_h.at[at + 2, :, part(slot * 128, 128)]
        return [
            pltpu.make_async_copy(W_h.at[at + slot], W.at[slot], sw.at[slot, 0]),
            pltpu.make_async_copy(half, Wd.at[slot], sw.at[slot, 1]),
        ]

    def gcp(c):
        at, slot = 4 + 3 * (c // 2), c % 2
        half = G_h.at[at + 2, :, part(slot * 128, 128)]
        return [
            pltpu.make_async_copy(G.at[slot], G_h.at[at + slot], sg.at[slot, 0]),
            pltpu.make_async_copy(Gd.at[slot], half, sg.at[slot, 1]),
        ]

    starts(wcp)(0)
    gacc[...] = jnp.zeros_like(gacc)
    for one in first:
        one.wait()

    def chunk(c, _):
        waits(wcp)(c)

        @pl.when(c < chunks - 1)
        def _next():
            starts(wcp)(c + 1)

        @pl.when(c >= 2)
        def _free():
            waits(gcp)(c - 2)

        slot = c % 2
        feed_chunk(n2, cot, W.at[slot], Wd.at[slot], G.at[slot], Gd.at[slot], hid, dgu, oacc, gacc)
        starts(gcp)(c)
        return 0

    lax.fori_loop(0, chunks, chunk, 0)
    n2[...] = oacc[...].astype(BF)
    c1 = pltpu.make_async_copy(n2, out_h, s.at[0])
    c1.start()
    feed_finish(gacc, mixed, cot, vec, vecs, oacc)
    c2 = pltpu.make_async_copy(oacc, gm_h, s.at[1])
    c3 = pltpu.make_async_copy(vecs, vecs_h, s.at[2])
    c2.start()
    c3.start()
    waits(gcp)(chunks - 2)
    waits(gcp)(chunks - 1)
    c1.wait()
    c2.wait()
    c3.wait()


def feed_finish(gacc, mixed, cot, vec, vecs, gm):
    vecs[...] = jnp.zeros_like(vecs)

    def block(r, _):
        rows = pl.ds(pl.multiple_of(r * BLK, BLK), BLK)
        hat, rstd = hat_of(mixed[rows, :])
        grad = gacc[rows, :]
        vecs[0:1, :] += jnp.sum(grad * hat, axis=0, keepdims=True)
        vecs[1:2, :] += jnp.sum(grad, axis=0, keepdims=True)
        gm[rows, :] = cot[rows, :].astype(F32) + norm_back(grad, hat, rstd, vec[2:3, :])
        return 0

    lax.fori_loop(0, mixed.shape[0] // BLK, block, 0)


def run_b(n2, cot, mixed, vec, W):
    T, D = n2.shape
    sds = jax.ShapeDtypeStruct
    half = D // 2
    return pl.pallas_call(
        kernel_b,
        name="feed_forward",
        out_shape=[sds((T, D), BF), sds((T, D), F32), sds((8, D), F32), sds(W.shape, BF)],
        in_specs=[ANY] * 5,
        out_specs=[ANY] * 4,
        scratch_shapes=[
            pltpu.VMEM((T, D), BF), pltpu.VMEM((T, D), BF), pltpu.VMEM((T, D), F32), pltpu.VMEM(vec.shape, F32),
            pltpu.VMEM((T, D), F32), pltpu.VMEM((T, D), F32), pltpu.VMEM((2, ZN, 256, D), BF), pltpu.VMEM((2, ZN, 128, D), BF),
            pltpu.VMEM((T, half), BF), pltpu.VMEM((T, D), BF), pltpu.VMEM((2, ZN, 256, D), BF), pltpu.VMEM((2, ZN, 128, D), BF),
            pltpu.VMEM((8, D), F32),
            pltpu.SemaphoreType.DMA((5,)), pltpu.SemaphoreType.DMA((2, 2)), pltpu.SemaphoreType.DMA((2, 2)),
        ],
        compiler_params=pltpu.CompilerParams(vmem_limit_bytes=62 * MIB),
    )(n2, cot, mixed, vec, W)


def attention_backward(j, pair, qaug, kaug, vaug, doaug, dq, dk, dv):
    T = qaug.shape[0]
    low, high = max(0, j - 1) * BLK, min(T, (j + 2) * BLK)
    keys = slice(j * BLK, (j + 1) * BLK)
    sums = []
    for one in range(2):
        cols = pl.ds(pl.multiple_of((2 * pair + one) * 128, 128), 128)
        prob = jnp.exp2(nt(kaug[keys, cols], qaug[low:high, cols]))
        grad = nt(vaug[keys, cols], doaug[low:high, cols])
        prob_low = prob.astype(BF)
        gs = (prob * grad).astype(BF)
        sums.append((
            nn(prob_low, doaug[low:high, cols]),
            nn(gs, qaug[low:high, cols]),
            tn(gs, kaug[keys, cols]),
        ))
    left = lanes((BLK, 128)) < HEAD
    dv[keys, :] = jnp.where(left, sums[0][0], sums[1][0])
    dk[keys, :] = jnp.where(left, sums[0][1], sums[1][1]) * (1.0 / LOG2E)
    left = lanes((high - low, 128)) < HEAD
    dq[low:high, :] += jnp.where(left, sums[0][2], sums[1][2]) * (1.0 / math.sqrt(HEAD))


def head_grads(gm, att, W, doaug):
    T, D = gm.shape

    def block(j, _):
        flat = nt(gm[...].astype(BF), W[j])
        lane = lanes((T, 128))
        left = lane < HEAD
        for p in range(2):
            grad = flat[:, 128 * p : 128 * p + 128].astype(BF).astype(F32)
            prod = grad * att[:, pl.ds(pl.multiple_of(j * 256 + 128 * p, 128), 128)].astype(F32)
            for one in range(2):
                own = left if one == 0 else lane >= HEAD
                dot = jnp.sum(jnp.where(own, prod, 0.0), axis=-1, keepdims=True)
                base = HEAD if one == 0 else 0
                kept = jnp.where(own, grad, 0.0)
                for k, part in enumerate(split_three(-dot)):
                    kept = jnp.where(lane == base + 8 + k, part, kept)
                at = (4 * j + 2 * p + one) * 128
                doaug[:, pl.ds(pl.multiple_of(at, 128), 128)] = kept.astype(BF)
        return 0

    lax.fori_loop(0, D // 256, block, 0)


def backward_pair(pair, qaug, kaug, vaug, doaug, dq, dk, dv, cos, sin, dqkv):
    T = qaug.shape[0]
    dq[...] = jnp.zeros_like(dq)
    for j in range(T // BLK):
        attention_backward(j, pair, qaug, kaug, vaug, doaug, dq, dk, dv)
    cols = pl.ds(pl.multiple_of(pair * 128, 128), 128)
    dqkv[0, :, cols] = unturn(dq[...], cos[...], sin[...]).astype(BF)
    dqkv[1, :, cols] = unturn(dk[...], cos[...], sin[...]).astype(BF)
    dqkv[2, :, cols] = dv[...].astype(BF)


def input_finish(gn1, x, gm, vec, vecs):
    vecs[...] = jnp.zeros_like(vecs)

    def rows_of(r, _):
        rows = pl.ds(pl.multiple_of(r * BLK, BLK), BLK)
        hat, rstd = hat_of(x[rows, :].astype(F32))
        grad = gn1[rows, :]
        vecs[0:1, :] += jnp.sum(grad * hat, axis=0, keepdims=True)
        vecs[1:2, :] += jnp.sum(grad, axis=0, keepdims=True)
        gm[rows, :] += norm_back(grad, hat, rstd, vec[0:1, :])
        return 0

    lax.fori_loop(0, x.shape[0] // BLK, rows_of, 0)


def kernel_c(
    tok_h, vec_h, cos_h, sin_h, W_h, gm_h, n1_h, att_h, qaug_h, kaug_h, vaug_h,
    ig_h, vecs_h, G_h,
    vec, cos, sin, W, gm, att, qaug, kaug, vaug, doaug, dq, dk, dv, n1, dqkv, gn1, G, vecs, sems, sw, sg,
):
    T, D = gm.shape
    first = copies(
        [
            (gm_h, gm), (att_h, att), (W_h.at[3], W.at[0]), (vec_h, vec), (cos_h, cos), (sin_h, sin),
            (qaug_h, qaug), (kaug_h, kaug), (vaug_h, vaug), (n1_h, n1),
        ],
        sems,
    )
    for one in first[:6]:
        one.wait()
    head_grads(gm, att, W.at[0], doaug)
    wcps = [pltpu.make_async_copy(W_h.at[k], W.at[k % 2], sw.at[k % 2]) for k in range(3)]
    wcps[0].start()
    wcps[1].start()
    G[0] = tn(att[...], gm[...].astype(BF)).astype(BF).reshape(ZN, D // ZN, D)
    gcps = [pltpu.make_async_copy(G.at[k % 2], G_h.at[(3, 0, 1, 2)[k]], sg.at[k % 2]) for k in range(4)]
    gcps[0].start()
    for one in first[6:]:
        one.wait()

    def per_pair(pair, _):
        backward_pair(pair, qaug, kaug, vaug, doaug, dq, dk, dv, cos, sin, dqkv)
        return 0

    lax.fori_loop(0, D // 128, per_pair, 0)
    tokc = pltpu.make_async_copy(tok_h, att, sems.at[0])
    tokc.start()
    for k in range(3):
        if k >= 1:
            gcps[k - 1].wait()
        G[(k + 1) % 2] = tn(n1[...], dqkv[k]).astype(BF).reshape(ZN, D // ZN, D)
        gcps[k + 1].start()
        wcps[k].wait()
        term = nt(dqkv[k], W[k % 2].reshape(D, D))
        gn1[...] = term if k == 0 else gn1[...] + term
        if k == 0:
            wcps[2].start()
    tokc.wait()
    input_finish(gn1, att, gm, vec, vecs)
    last = copies([(gm, ig_h), (vecs, vecs_h)], sems)
    gcps[2].wait()
    gcps[3].wait()
    for one in last:
        one.wait()


def run_c(tok, vec, cos, sin, W, gm, n1, att, qaug, kaug, vaug):
    T, D = tok.shape
    sds = jax.ShapeDtypeStruct
    v = pltpu.VMEM
    return pl.pallas_call(
        kernel_c,
        name="attention_backward",
        out_shape=[sds((T, D), F32), sds((8, D), F32), sds((4, ZN, D // ZN, D), BF)],
        in_specs=[ANY] * 11,
        out_specs=[ANY] * 3,
        scratch_shapes=[
            v(vec.shape, F32), v((T, 128), F32), v((T, 128), F32), v((2, ZN, D // ZN, D), BF), v((T, D), F32), v((T, D), BF),
            v((T, 2 * D), BF), v((T, 2 * D), BF), v((T, 2 * D), BF), v((T, 2 * D), BF),
            v((T, 128), F32), v((T, 128), F32), v((T, 128), F32), v((T, D), BF), v((3, T, D), BF), v((T, D), F32),
            v((2, ZN, D // ZN, D), BF), v((8, D), F32),
            pltpu.SemaphoreType.DMA((10,)), pltpu.SemaphoreType.DMA((2,)), pltpu.SemaphoreType.DMA((2,)),
        ],
        compiler_params=pltpu.CompilerParams(vmem_limit_bytes=62 * MIB),
    )(tok, vec, cos, sin, W, gm, n1, att, qaug, kaug, vaug)


def tables(lengths, row_len):
    order = jnp.arange(lengths.shape[-1], dtype=jnp.int32)
    ends = jnp.sum(jnp.where(order[:, None] <= order[None, :], lengths[0][:, None], 0), axis=0)
    starts = ends - lengths[0]
    places = jnp.arange(row_len, dtype=jnp.int32)[:, None]
    inside = (places >= starts[None, :]) & (places < ends[None, :])
    offset = jnp.sum(jnp.where(inside, starts[None, :], 0), axis=1, keepdims=True)
    lane = jnp.arange(128, dtype=jnp.int32)
    power = (lane % (HEAD // 2)).astype(F32) * (-2.0 / HEAD)
    inverse = jnp.power(jnp.float32(ROTARY_BASE), power)
    angles = (places - offset).astype(F32) * inverse[None, :]
    sign = jnp.where(lane % HEAD < HEAD // 2, -1.0, 1.0).astype(F32)
    place = lane % HEAD
    mine = jnp.sum(
        jnp.where(inside[:, None, :] & (order[None, None, :] == place[None, :, None]), 1.0, 0.0), axis=-1
    )
    aq = mine.astype(BF)
    ak = jnp.where(place < 8, (mine - 1.0) * 1e30, jnp.where(place < 11, 1.0, 0.0)).astype(BF)
    return jnp.cos(angles), jnp.sin(angles) * sign[None, :], aq, ak


def kernel_spread(fin_h, q_h, k_h, v_h, o_h, gate_h, up_h, down_h, fin, wide, sems, osems):
    n = fin_h.shape[0]
    load = [pltpu.make_async_copy(fin_h.at[p], fin.at[p], sems.at[p]) for p in range(n)]
    for copy in load:
        copy.start()
    out = []
    for p in range(n):
        load[p].wait()
        wide[p] = fin[p].astype(F32)
        made = []
        if p < 4:
            made.append((wide.at[p], (q_h, k_h, v_h, o_h)[p]))
        elif (p - 4) % 3 == 2:
            made.append((wide.at[p], down_h.at[pl.ds(256 * ((p - 4) // 3), 256)]))
        else:
            i = 2 * ((p - 4) // 3) + (p - 4) % 3
            for j in range(ZN):
                cols = pl.ds(1024 * j + 128 * i, 128)
                made.append((wide.at[p, :, pl.ds(128 * j, 128)], gate_h.at[:, cols]))
                made.append((wide.at[p, :, pl.ds(512 + 128 * j, 128)], up_h.at[:, cols]))
        out += [pltpu.make_async_copy(x, y, osems.at[p, i]) for i, (x, y) in enumerate(made)]
        for copy in out[-len(made) :]:
            copy.start()
    for copy in out:
        copy.wait()


def run_spread(fin, shapes):
    return pl.pallas_call(
        kernel_spread,
        name="spread_sums",
        out_shape=[jax.ShapeDtypeStruct(shape, F32) for shape in shapes],
        in_specs=[ANY],
        out_specs=[ANY] * len(shapes),
        scratch_shapes=[
            pltpu.VMEM(fin.shape, BF), pltpu.VMEM(fin.shape, F32),
            pltpu.SemaphoreType.DMA((16,)), pltpu.SemaphoreType.DMA((16, 8)),
        ],
        compiler_params=pltpu.CompilerParams(vmem_limit_bytes=40 * MIB),
    )(fin)


def sum_rest(part_sum):
    size, step = lax.axis_size("wide"), 8
    while step < size:
        pairs = [(i, (i // (2 * step)) * 2 * step + (i + step) % (2 * step)) for i in range(size)]
        other = lax.ppermute(part_sum, "wide", pairs)
        part_sum = (part_sum.astype(F32) + other.astype(F32)).astype(part_sum.dtype)
        step *= 2
    return part_sum


def shards(
    tokens, lengths, ln1_gain, ln1_bias, w_query, w_key, w_value, w_out,
    ln2_gain, ln2_bias, w_gate, w_up, w_down, cotangent,
):
    _rows, T, D = tokens.shape
    DR = D // ZN
    vectors = lax.all_gather(jnp.stack([ln1_gain, ln1_bias, ln2_gain, ln2_bias]), "narrow", axis=1, tiled=True)
    vec = jnp.concatenate([vectors.astype(F32), jnp.zeros((4, D), F32)])
    cos, sin, aq, ak = tables(lengths, T)
    W = run_gather(w_query, w_key, w_value, w_out, w_gate, w_up, w_down)
    tok, cot = tokens[0], cotangent[0]
    mixed, n2, n1, att, qaug, kaug, vaug = run_a(tok, vec, cos, sin, aq, ak, W)
    out, gm, vecs2, G_ffn = run_b(n2, cot, mixed, vec, W)
    input_grad, vecs1, G_attn = run_c(tok, vec, cos, sin, W, gm, n1, att, qaug, kaug, vaug)
    fin = sum_rest(run_reduce(G_attn, G_ffn))
    sums = run_spread(fin, [w.shape for w in (w_query, w_key, w_value, w_out, w_gate, w_up, w_down)])
    vector_sums = lax.psum(jnp.concatenate([vecs1[:2], vecs2[:2]]), ("wide", "narrow"))
    mine = lax.dynamic_slice_in_dim(vector_sums, lax.axis_index("narrow") * DR, DR, axis=1)
    return (out[None], input_grad[None], mine[0], mine[1], *sums[:4], mine[2], mine[3], *sums[4:])


def solution(mesh):
    both = ("wide", "narrow")
    row3, row2, vector, matrix = P(both, None, None), P(both, None), P("narrow"), P("narrow", None)
    weights = (vector, vector, matrix, matrix, matrix, matrix, vector, vector, matrix, matrix, matrix)
    return jax.shard_map(
        shards,
        mesh=mesh,
        in_specs=(row3, row2) + weights + (row3,),
        out_specs=(row3, row3) + weights,
        check_vma=False,
    )
```

time: 1200 us -> 622 us (0.52)
  Pallas kernels: 0 us -> 543 us
  matrix products: 407 us -> 0 us
  waiting for transfers between devices: 379 us -> 0 us
  local copies, waits for them, and re-layouts: 176 us -> 9.82 us
  other arithmetic: 152 us -> 12.8 us
  between operations: 15 us -> 1.02 us
    pallas_call x0 -> x6, Pallas kernels: none -> 543 us  [the longest x1 189 us: run_reduce(): pl.pallas_call(kernel_reduce, name='gradient_sums', out_shape=jax.ShapeDt...]
    dot_general x35 -> x0, matrix products: 407 us -> none  [the longest x4 59.9 us: masked_scores(): jnp.einsum('qhe,khe->hqk', query_block, keys_row, preferred_element_type=...]
    reduce_scatter x3 -> x0, waiting for transfers between devices: 296 us -> none  [sum_shards(): lax.psum_scatter(grad.astype(jnp.bfloat16), ('narrow', 'wide'), scatter_d...]
    dynamic_update_slice x4 -> x0, local copies, waits for them, and re-layouts: 83.3 us -> none  [attend_row(): lax.map(one_block, (split_blocks(queries_row), split_blocks(segment_row)))]
    all_gather x6 -> x0, waiting for transfers between devices: 82.3 us -> none  [the longest x3 76.7 us: gather_whole(): return lax.all_gather(piece, ('narrow', 'wide'), axis=0, tiled=True)]
    convert_element_type x12 -> x3, other arithmetic: 80.1 us -> 1.52 us  [the longest x1 0.78 us: tables(): jnp.where(place < 8, (mine - 1.0) * 1e+30, jnp.where(place < 11, 1.0, 0.0))]
    unnamed x116 -> x22, local copies, waits for them, and re-layouts: 46.5 us -> 7.36 us
    reduce_sum x7 -> x3, other arithmetic: 32.9 us -> 6.79 us  [the longest x1 5.82 us: tables(): jnp.sum(jnp.where(inside[:, None, :] & (order[None, None, :] == place[Non...]
  transfers between devices with their start and end apart: 9 -> 0, of which waited for: 5 -> 0; matrix products, arithmetic and copies ran while one was open for 52% -> 0% of each run, Pallas kernels for 0% -> 0%
where the time goes in v2:
time: 622 us; the launch traced here: 618 us
  Pallas kernels  543 us (87%)
  blocking collectives  51.7 us (8%)
  other arithmetic  12.8 us (2%)
  local copies, waits for them, and re-layouts  9.82 us (2%)
    pallas_call x1, Pallas kernels, run_reduce(): pl.pallas_call(kernel_reduce, name='gradient_sums', out_shape=jax.ShapeDt...  189 us
    pallas_call x1, Pallas kernels, run_gather(): pl.pallas_call(kernel_gather, name='weights', out_shape=jax.ShapeDtypeStr...  139 us
    pallas_call x1, Pallas kernels, run_b(): pl.pallas_call(kernel_b, name='feed_forward', out_shape=[sds((T, D), BF),...  92.4 us
    pallas_call x1, Pallas kernels, run_c(): pl.pallas_call(kernel_c, name='attention_backward', out_shape=[sds((T, D)...  64 us
    pallas_call x1, Pallas kernels, run_a(): pl.pallas_call(kernel_a, name='attention_forward', out_shape=[sds((T, D),...  51.1 us
    psum x1, blocking collectives, shards(): lax.psum(jnp.concatenate([vecs1[:2], vecs2[:2]]), ('wide', 'narrow'))  39.1 us
    all_gather x1, blocking collectives, shards(): lax.all_gather(jnp.stack([ln1_gain, ln1_bias, ln2_gain, ln2_bias]), 'narr...  12.6 us

profile of v2, /device:TPU:0, one launch (start us, length us, event | category | flops | bytes accessed | tf_op | source)
XLA Modules:
  0.0 617.8 jit_solution(3355824846738058943)
XLA Ops:
  0.6 0.0 copy-start
  0.7 0.9 select_reduce_fusion.2
  1.5 0.7 fusion.5
  2.2 0.1 select_reduce_fusion.1
  2.3 3.1 fusion
  5.4 0.1 fusion.1
  5.5 0.3 copy.27
  5.8 5.8 select_reduce_fusion
  11.6 0.8 select_convert_fusion.ak_h
  12.4 0.7 convert_element_type.24.aq_h
  13.1 0.0 copy-done
  13.1 0.0 copy-start.1
  13.1 1.6 copy-done.1
  14.7 0.0 copy-start.2
  14.7 1.6 copy-done.2
  16.3 0.0 copy-start.3
  16.3 1.0 copy-done.3
  17.3 0.0 copy-start.4
  17.3 1.0 copy-done.4
  18.4 0.0 copy-start.5
  18.4 1.0 copy-done.5
  19.4 0.0 copy-start.6
  19.4 1.0 copy-done.6
  20.5 0.0 copy-start.7
  20.5 0.0 copy-start.8
  20.5 0.0 copy-start.9
  20.5 0.0 copy-start.10
  20.5 138.8 %weights.1.W_h = bf16[16,4,256,1024]{3,2,1,0:T(8,128)(2,1)} custom-call(bf16[256,1024]{1,0:T(8,128)(2,1)S(1)} %copy-done.3, bf16[256,1024]{1,0:T(8,128)(2,1)S(1)} %copy-done.4, bf16[256,1024]{1,0:T(8,128)(2,1)S(1)} %copy-done.5, bf16[256,1024]{1,0:T(8,128)(2,1)S(1)} %copy-done.6, bf16[256,4096]{1,0:T(8,128)(2,1)S(1)} %copy-done, ...), custom_call_target="tpu_custom_call" | custom-call | tf_op jit(solution)/shard_map/weights/pallas_call | solution.py:358
  159.2 0.0 copy-done.7
  159.3 0.0 copy-done.8
  159.3 0.0 copy-done.9
  159.3 0.0 copy-done.10
  159.4 12.6 %all_gather.3 = bf16[4,1024]{1,0:T(4,128)(2,1)S(1)} all-gather(bf16[4,256]{1,0:T(4,128)(2,1)S(1)} %pad_maximum_fusion.1), channel_id=1, replica_groups=mesh['wide'=8,'narrow'=4] {'narrow'}, dimensions={1}, use_global_device_ids=true | all-gather | bytes 10240 | tf_op jit(solution)/shard_map/all_gather | solution.py:907
  171.9 0.6 pad_convert_fusion.vec_h
  172.5 51.1 %attention_forward.1 = (f32[1024,1024]{1,0:T(8,128)}, bf16[1024,1024]{1,0:T(8,128)(2,1)}, bf16[1024,1024]{1,0:T(8,128)(2,1)}, bf16[1024,1024]{1,0:T(8,128)(2,1)}...) custom-call(bf16[1024,1024]{1,0:T(8,128)(2,1)} %bitcast.15, ...), custom_call_target="tpu_custom_call" | custom-call | tf_op jit(solution)/shard_map/attention_forward/pallas_call | solution.py:547
  223.6 92.4 %feed_forward.1 = (bf16[1024,1024]{1,0:T(8,128)(2,1)}, f32[1024,1024]{1,0:T(8,128)}, f32[8,1024]{1,0:T(8,128)}, bf16[16,4,256,1024]{3,2,1,0:T(8,128)(2,1)}) custom-call(bf16[1024,1024]{1,0:T(8,128)(2,1)} %get-tuple-element.34.n2_h, bf16[1024,1024]{1,0:T(8,128)(2,1)} %bitcast.17, f32[1024,1024]{1,0:T(8,128)} %get-tuple-element.35.mixed_h, ...), custom_call_target="tpu_custom_call" | custom-call | tf_op jit(solution)/shard_map/feed_forward/pallas_call | solution.py:666
  316.0 64.0 %attention_backward.1 = (f32[1024,1024]{1,0:T(8,128)}, f32[8,1024]{1,0:T(8,128)}, bf16[4,4,256,1024]{3,2,1,0:T(8,128)(2,1)}) custom-call(bf16[1024,1024]{1,0:T(8,128)(2,1)} %bitcast.16, f32[8,1024]{1,0:T(8,128)} %pad_convert_fusion.vec_h, f32[1024,128]{1,0:T(8,128)} %get-tuple-element.60.cos_h, f32[1024,128]{1,0:T(8,128)} %get-tuple-element.59.sin_h, ...), custom_call_target="tpu_custom_call" | custom-call | tf_op jit(solution)/shard_map/attention_backward/pallas_call | solution.py:811
  380.0 188.6 %gradient_sums.1.fin_h = bf16[16,256,1024]{2,1,0:T(8,128)(2,1)S(1)} custom-call(bf16[4,4,256,1024]{3,2,1,0:T(8,128)(2,1)} %get-tuple-element.46.Ga_h, bf16[16,4,256,1024]{3,2,1,0:T(8,128)(2,1)} %get-tuple-element.47.G_h), custom_call_target="tpu_custom_call" | custom-call | tf_op jit(solution)/shard_map/gradient_sums/pallas_call | solution.py:411
  568.7 7.7 %spread_sums.1 = (f32[256,1024]{1,0:T(8,128)}, f32[256,1024]{1,0:T(8,128)}, f32[256,1024]{1,0:T(8,128)}, f32[256,1024]{1,0:T(8,128)}, f32[256,4096]{1,0:T(8,128)...) custom-call(bf16[16,256,1024]{2,1,0:T(8,128)(2,1)S(1)} %gradient_sums.1.fin_h), custom_call_target="tpu_custom_call" | custom-call | tf_op jit(solution)/shard_map/spread_sums/pallas_call | solution.py:877
  576.4 0.8 slice.18
  577.1 0.8 slice.19
  577.9 39.1 %psum.7 = f32[4,1024]{1,0:T(4,128)S(1)} all-reduce(f32[4,1024]{1,0:T(4,128)S(1)} %pad_maximum_fusion), channel_id=1, replica_groups=mesh['wide'=8,'narrow'=4] {'wide','narrow'}, use_global_device_ids=true, to_apply=%region_3.4 | all-reduce | flops 4096 | bytes 32768 | tf_op jit(solution)/shard_map/psum | solution.py:917
  617.0 0.6 fusion.6
  (12 shorter events, 0.1 us)
Async XLA Ops:
  0.6 12.5 %copy-start = (bf16[256,4096]{1,0:T(8,128)(2,1)S(1)}, bf16[256,4096]{1,0:T(8,128)(2,1)}, u32[]{:S(2)}) copy-start(bf16[256,4096]{1,0:T(8,128)(2,1)} %gate.1) | copy-start | bytes 6291460
  13.1 1.6 copy-start.1
  14.7 1.6 copy-start.2
  16.3 1.0 copy-start.3
  17.3 1.0 copy-start.4
  18.4 1.0 copy-start.5
  19.4 1.0 copy-start.6
  20.5 138.8 %copy-start.7 = (bf16[256]{0:T(256)(128)(2,1)S(1)}, bf16[256]{0:T(256)(128)(2,1)}, u32[]{:S(2)}) copy-start(bf16[256]{0:T(256)(128)(2,1)} %param.16) | copy-start | bytes 1540
  20.5 138.8 %copy-start.8 = (bf16[256]{0:T(256)(128)(2,1)S(1)}, bf16[256]{0:T(256)(128)(2,1)}, u32[]{:S(2)}) copy-start(bf16[256]{0:T(256)(128)(2,1)} %param.17) | copy-start | bytes 1540
  20.5 138.8 %copy-start.9 = (bf16[256]{0:T(256)(128)(2,1)S(1)}, bf16[256]{0:T(256)(128)(2,1)}, u32[]{:S(2)}) copy-start(bf16[256]{0:T(256)(128)(2,1)} %param.22) | copy-start | bytes 1540
  20.5 138.8 %copy-start.10 = (bf16[256]{0:T(256)(128)(2,1)S(1)}, bf16[256]{0:T(256)(128)(2,1)}, u32[]{:S(2)}) copy-start(bf16[256]{0:T(256)(128)(2,1)} %param.23) | copy-start | bytes 1540
